TPU v7x, 256 devices: a whole 4x4x8 slice. The times are simulated.
256 devices in a mesh: pair: 64 (over z, x, core), aux: 4 (over y).
Axes of the slice: x: 4, y: 4, z: 8, core: 2. Of those that a mesh axis runs over, the one named last changes fastest.
Arguments:
- ao_blocks: bfloat16 [64, 64, 16, 128, 128], P(None, 'pair', 'aux'), may hold values from -6 to 6
- block_live: int32 [64, 64], replicated, may hold values from 0 to 1, as said below
- tile_len: int32 [64], replicated, may hold values from 1 to 128, 6000 in all
- coeffs: bfloat16 [8192, 576], P('pair'), may hold values from -0.078125 to 0.078125
- metric_panel: bfloat16 [16, 32], replicated, may hold values from -1.5 to 1.5
Outputs:
- fitted: bfloat16 [32, 576, 8192], P('aux', 'pair')
Inputs may be any that keep to these rules, and one draw needn't show every extreme that they name: `block_live`: entries with row block before column block are 0; the diagonal and the two block diagonals below it are 1. `tile_len`: the counts sum to 6000; some shell block holds exactly 128.
All inputs are finite; a program needn't handle non-finite values.
Results may differ from a plain program's by a relative error of at most 0.0049.
Values may be sent and summed in bfloat16 or wider, within the bound.
A program may use at most 128 MiB of HBM per device.

v0:
```python
import jax
import jax.numpy as jnp
from jax import lax
from jax.sharding import PartitionSpec as P


def receive_rows(ao_blocks, tile_ids, columns, half_size):
    received = lax.all_to_all(ao_blocks, "pair", split_axis=0, concat_axis=1, tiled=True)
    source_upper = (tile_ids[None, :] > columns[:, None])[:, :, None, None, None]
    return jnp.where(
        source_upper, received[:, :, :, half_size:, :], received[:, :, :, :half_size, :]
    )


def shards(ao_blocks, block_live, tile_len, coeffs, metric_panel):
    tile_count = ao_blocks.shape[0]
    own_count = ao_blocks.shape[1]
    slab_count = ao_blocks.shape[2]
    slot_size = ao_blocks.shape[3]
    half_size = slot_size // 2
    occ_count = coeffs.shape[1]
    first_tile = lax.axis_index("pair") * own_count
    tile_ids = jnp.arange(tile_count, dtype=jnp.int32)
    columns = first_tile + jnp.arange(own_count, dtype=jnp.int32)
    inside = jnp.arange(slot_size, dtype=jnp.int32)
    upper_rows = inside >= half_size
    lower_half = inside[:, None] >= inside[None, :]
    strict_lower = inside[:, None] > inside[None, :]
    kept_blocks = (block_live > 0) & (tile_ids[:, None] >= tile_ids[None, :])
    valid_slots = inside[None, :] < tile_len[:, None]
    valid_columns = lax.dynamic_slice_in_dim(valid_slots, first_tile, own_count, 0)
    kept_own = lax.dynamic_slice_in_dim(kept_blocks, first_tile, own_count, 1)
    kept_across = lax.dynamic_slice_in_dim(kept_blocks, first_tile, own_count, 0)
    later_tiles = tile_ids[:, None] > columns[None, :]
    same_tile = tile_ids[:, None] == columns[None, :]
    earlier_tiles = columns[:, None] > tile_ids[None, :]
    same_across = columns[:, None] == tile_ids[None, :]
    own_mask = (
        kept_own[:, :, None, None]
        & (later_tiles[:, :, None, None] | same_tile[:, :, None, None] & lower_half[None, None])
        & valid_slots[:, None, :, None]
        & valid_columns[None, :, None, :]
    )
    across_mask = (
        kept_across[:, :, None, None]
        & (
            earlier_tiles[:, :, None, None]
            | same_across[:, :, None, None] & strict_lower[None, None]
        )
        & valid_columns[:, None, :, None]
        & valid_slots[None, :, None, :]
    )
    upper_four = upper_rows[None, None, :, None]
    mask_stored = own_mask & jnp.logical_not(later_tiles[:, :, None, None] & upper_four)
    across_turned = jnp.transpose(across_mask, (1, 0, 2, 3))
    mask_mirror = across_turned & (
        jnp.transpose(earlier_tiles)[:, :, None, None] & upper_four | same_tile[:, :, None, None]
    )
    own_turned = jnp.transpose(own_mask, (1, 0, 2, 3))
    mask_arrived = own_turned[:, :, half_size:, :] & jnp.transpose(later_tiles)[:, :, None, None]
    mask_crossed = across_mask[:, :, :half_size, :] & earlier_tiles[:, :, None, None]
    zero_value = jnp.zeros((), ao_blocks.dtype)
    own_stored = jnp.where(mask_stored[:, :, None], ao_blocks, zero_value)
    own_mirror = jnp.where(mask_mirror[:, :, None], ao_blocks, zero_value)
    received = receive_rows(ao_blocks, tile_ids, columns, half_size)
    arrived = jnp.where(mask_arrived[:, :, None], received, zero_value)
    crossed = jnp.where(mask_crossed[:, :, None], received, zero_value)
    coef_rows = lax.all_gather(coeffs, "pair", axis=0, tiled=True)
    tile_span = coef_rows.shape[0] // slot_size
    coef_piece = coef_rows.reshape(tile_span, slot_size, occ_count)
    first = jnp.einsum(
        "kri,kgprs->pigs", coef_piece, own_stored, preferred_element_type=jnp.float32
    )
    partial_sum = first + jnp.einsum(
        "ksi,kgprs->pigr", coef_piece, own_mirror, preferred_element_type=jnp.float32
    )
    first = jnp.einsum(
        "kri,gkprs->pigs", coef_piece[:, half_size:, :], arrived, preferred_element_type=jnp.float32
    )
    lower_rows = jnp.einsum(
        "ksi,gkprs->pigr", coef_piece, crossed, preferred_element_type=jnp.float32
    )
    padding = jnp.zeros(lower_rows.shape[:3] + (slot_size - half_size,), jnp.float32)
    running = partial_sum + (first + jnp.concatenate([lower_rows, padding], axis=3))
    half_done = running.astype(jnp.bfloat16).reshape(slab_count, occ_count, own_count * slot_size)
    regrouped = lax.all_to_all(half_done, "pair", split_axis=1, concat_axis=2, tiled=True)
    slab_metric = lax.dynamic_slice_in_dim(
        metric_panel, lax.axis_index("aux") * slab_count, slab_count, 0
    )
    fitted = lax.psum_scatter(
        jnp.einsum("pq,pin->qin", slab_metric, regrouped, preferred_element_type=jnp.float32),
        "aux",
        scatter_dimension=0,
        tiled=True,
    )
    return fitted.astype(jnp.bfloat16)


def solution(mesh):
    in_specs = (P(None, "pair", "aux", None, None), P(), P(), P("pair", None), P())
    out_specs = P("aux", "pair", None)
    return jax.shard_map(shards, mesh=mesh, in_specs=in_specs, out_specs=out_specs, check_vma=False)
```

profile of v0, /device:TPU:1, one launch (start us, length us, event | category | flops | bytes accessed | tf_op | source)
XLA Modules:
  0.0 427.0 jit_solution(2690631883624345564)
XLA Ops:
  6.5 0.0 copy-start
  6.5 0.7 all-gather.2.cloned.1.call-update
  7.3 0.0 copy-start.3
  7.3 0.0 copy-start.2
  7.3 13.3 %all-to-all-start = ((bf16[64,1,4,128,128]{4,3,2,1,0:T(8,128)(2,1)}), bf16[64,1,4,128,128]{4,3,2,1,0:T(8,128)(2,1)}, u32[]{:S(2)}, u32[]{:S(2)}) async-start(bf16[64,1,4,128,128]{4,3,2,1,0:T(8,128)(2,1)} %param.5), calls=%async_computation | async-start | bytes 16777216 | tf_op jit(solution)/shard_map/all_to_all | solution.py:8
  20.6 0.1 iota_compare_fusion.2
  20.7 0.1 slice.21
  20.9 0.2 dynamic-slice_reduce_fusion
  21.1 0.1 and_or_fusion
  21.2 2.5 and_bitcast_fusion
  23.7 1.2 and_bitcast_fusion.1
  24.9 4.9 %and_and_fusion = (pred[64,128,128]{2,1,0:T(8,128)(4,1)S(1)}, pred[64,128,128]{2,1,0:T(8,128)(4,1)S(1)}) fusion(pred[128]{0:T(512)(128)(4,1)S(1)} %dynamic-slice_bitcast_fusion.1, pred[64]{0:T(512)(128)(4,1)S(1)} %get-tuple-element.10, pred[64]{0:T(512)(128)(4,1)S(1)} %dynamic-slice_bitcast_fusion, pred[64,128]{1,0:T(8,128)(4,1)S(1)} %get-tuple-element.7, ...), kind=kLoop, calls=%fused_computation.23 | loop fusion | flops 12582912 | bytes 2155008 | tf_op jit(solution)/shard_map/and | solution.py:56
  29.8 177.4 %all-gather.2.cloned.1.call-done = bf16[8192,576]{0,1:T(8,128)(2,1)} async-done(((bf16[128,576]{0,1:T(8,128)(2,1)}), bf16[8192,576]{0,1:T(8,128)(2,1)}) %all-gather.2.cloned.1.call-update) | async-done | bytes 9437200 | tf_op jit(solution)/shard_map/all_gather | solution.py:68
  207.2 10.4 %copy.45 = bf16[72,8,64,128]{3,2,1,0:T(8,128)(2,1)} copy(bf16[72,8,64,128]{3,1,2,0:T(8,128)(2,1)} %bitcast.113) | data formatting | bytes 18874368
  217.6 10.4 %slice.24 = bf16[64,64,576]{1,0,2:T(8,128)(2,1)} slice(bf16[64,128,576]{1,0,2:T(8,128)(2,1)} %bitcast.107), slice={[0:64], [64:128], [0:576]} | slice | bytes 9437184 | tf_op jit(solution)/shard_map/slice | solution.py:78
  228.0 13.9 %copy.43 = bf16[64,64,576]{2,1,0:T(8,128)(2,1)} copy(bf16[64,64,576]{1,0,2:T(8,128)(2,1)} %slice.24) | data formatting | bytes 9437184
  241.9 10.4 %fusion.39 = f32[4,128,576]{1,2,0:T(8,128)} fusion(bf16[64,1,4,128,128]{4,3,2,1,0:T(8,128)(2,1)} %param.5, pred[64,128,128]{2,1,0:T(8,128)(4,1)S(1)} %get-tuple-element.6, bf16[64,128,576,1]{1,0,2,3:T(8,128)(2,1)} %bitcast.108), kind=kOutput, calls=%fused_computation.32 | convolution fusion | flops 4836032512 | bytes 20054016 | tf_op jit(solution)/shard_map/kri,kgprs->pigs/dot_general | solution.py:71
  252.3 0.0 all-to-all-done
  252.3 0.0 slice-start.1
  252.3 15.6 %fusion.34 = f32[4,576,1,64]{3,1,0,2:T(8,128)S(1)} fusion(bf16[64,128,576,1]{1,0,2,3:T(8,128)(2,1)} %bitcast.109, pred[64,64,128]{2,1,0:T(8,128)(4,1)S(1)} %and_bitcast_fusion, bf16[1,64,4,128,128]{4,3,2,1,0:T(8,128)(2,1)} %bitcast.12, pred[64]{0:T(512)(128)(4,1)S(1)} %iota_compare_fusion.8), kind=kOutput, calls=%fused_computation.31 | convolution fusion | flops 2420113408 | bytes 18939968 | tf_op jit(solution)/shard_map/ksi,gkprs->pigr/dot_general | solution.py:80
  268.0 0.0 slice-start.2
  268.0 7.4 %fusion.59 = f32[4,576,1,128]{3,1,0,2:T(8,128)} fusion(bf16[64,64,576]{2,1,0:T(8,128)(2,1)S(1)} %copy-done.1, pred[64,64,128]{2,1,0:T(8,128)(4,1)S(1)} %and_bitcast_fusion.1, f32[4,576,1,64]{3,1,0,2:T(8,128)S(1)} %fusion.34, bf16[1,64,4,128,128]{4,3,2,1,0:T(8,128)(2,1)} %bitcast.12, pred[64]{0:T(512)(128)(4,1)S(1)} %iota_compare_fusion.8), kind=kOutput, calls=%fused_computation.36 | convolution fusion | flops 2420408320 | bytes 15401024 | tf_op jit(solution)/shard_map/kri,gkprs->pigs/dot_general | solution.py:77
  275.4 0.0 slice-done.2
  275.4 14.4 %fusion.69 = bf16[4,576,128]{2,1,0:T(8,128)(2,1)S(1)} fusion(f32[4,576,1,128]{3,1,0,2:T(8,128)} %fusion.59, f32[4,128,576]{1,2,0:T(8,128)} %fusion.39, bf16[64,128,576,1]{1,0,2,3:T(8,128)(2,1)S(1)} %bitcast.112, bf16[64,1,4,128,128]{4,3,2,1,0:T(8,128)(2,1)} %param.5, pred[64,128,128]{2,1,0:T(8,128)(4,1)S(1)} %get-tuple-element.5), kind=kOutput, calls=%fused_computation.38 | convolution fusion | flops 4836917248 | bytes 21823488 | tf_op jit(solution)/shard_map/ksi,kgprs->pigr/dot_general | solution.py:74
  289.9 1.3 copy.29
  291.2 14.2 %all-to-all-start.1 = ((bf16[4,576,128]{2,0,1:T(4,128)(2,1)}), bf16[4,576,128]{2,0,1:T(4,128)(2,1)S(1)}, u32[]{:S(2)}, u32[]{:S(2)}) async-start(bf16[4,576,128]{2,0,1:T(4,128)(2,1)} %copy.29), calls=%async_computation.1 | async-start | bytes 1179648 | tf_op jit(solution)/shard_map/all_to_all | solution.py:86
  305.3 0.0 reduce-scatter.2.cloned.1.call-start
  305.4 19.0 %all-to-all-done.1 = bf16[4,576,128]{2,0,1:T(4,128)(2,1)S(1)} async-done(((bf16[4,576,128]{2,0,1:T(4,128)(2,1)}), bf16[4,576,128]{2,0,1:T(4,128)(2,1)S(1)}, u32[]{:S(2)}, u32[]{:S(2)}) %all-to-all-start.1) | async-done | bytes 589856 | tf_op jit(solution)/shard_map/all_to_all | solution.py:86
  324.4 4.5 %fusion.74 = f32[32,9,8192]{2,0,1:T(8,128)} fusion(bf16[64,9,1,4,128]{4,3,2,1,0:T(4,128)(2,1)S(1)} %bitcast.114, bf16[16,32]{1,0:T(8,128)(2,1)S(1)} %copy-done, s32[]{:T(128)S(6)} %select_n.26), kind=kOutput, calls=%fused_computation.39 | convolution fusion | flops 18874368 | bytes 10028036 | tf_op jit(solution)/shard_map/pq,pin->qin/dot_general | solution.py:91
  328.8 0.0 reduce-scatter.2.cloned.1.call-update
  328.9 88.5 %reduce-scatter.2.cloned.1.call-done = f32[8,9,8192]{2,0,1:T(8,128)} async-done(((f32[32,9,8192]{2,0,1:T(8,128)}), f32[8,9,8192]{2,0,1:T(8,128)}) %reduce-scatter.2.cloned.1.call-update) | async-done | bytes 2359312 | tf_op jit(solution)/shard_map/reduce_scatter | solution.py:90
  417.4 2.8 convert_element_type.7
  (20 shorter events, 0.1 us)
Async XLA Ops:
  6.5 317.9 %copy-start = (bf16[16,32]{1,0:T(8,128)(2,1)S(1)}, bf16[16,32]{1,0:T(8,128)(2,1)}, u32[]{:S(2)}) copy-start(bf16[16,32]{1,0:T(8,128)(2,1)} %param.9) | copy-start | bytes 3076
  6.5 200.6 %all-gather.2.cloned.1.call-start = ((), (), s32[]{:S(2)}) async-start(), calls=%async_computation.3 | async-start | bytes 9584640 | tf_op jit(solution)/shard_map/all_gather | solution.py:68
  7.3 13.4 %copy-start.3 = (s32[64]{0:T(128)S(1)}, s32[64]{0:T(128)}, u32[]{:S(2)}) copy-start(s32[64]{0:T(128)} %param.7) | copy-start | bytes 772
  7.3 13.6 %copy-start.2 = (s32[64,64]{1,0:T(8,128)S(1)}, s32[64,64]{1,0:T(8,128)}, u32[]{:S(2)}) copy-start(s32[64,64]{1,0:T(8,128)} %param.6) | copy-start | bytes 49156
  7.3 245.0 %all-to-all-start = ((bf16[64,1,4,128,128]{4,3,2,1,0:T(8,128)(2,1)}), bf16[64,1,4,128,128]{4,3,2,1,0:T(8,128)(2,1)}, u32[]{:S(2)}, u32[]{:S(2)}) async-start(bf16[64,1,4,128,128]{4,3,2,1,0:T(8,128)(2,1)} %param.5), calls=%async_computation | async-start | bytes 16777216 | tf_op jit(solution)/shard_map/all_to_all | solution.py:8
  252.3 15.7 %copy-start.1 = (bf16[64,64,576]{2,1,0:T(8,128)(2,1)S(1)}, bf16[64,64,576]{2,1,0:T(8,128)(2,1)}, u32[]{:S(2)}) copy-start(bf16[64,64,576]{2,1,0:T(8,128)(2,1)} %copy.43) | copy-start | bytes 14155780
  252.3 23.1 %slice-start = ((s8[9437184]{0:T(1024)(128)(4,1)}), s8[4194304]{0:T(1024)(128)(4,1)S(1)}, s32[]{:S(2)}) async-start(s8[9437184]{0:T(1024)(128)(4,1)} %bitcast.110), calls=%async_computation.5 | async-start | bytes 8388608
  252.3 23.1 %slice-start.1 = ((s8[9437184]{0:T(1024)(128)(4,1)}), s8[4194304]{0:T(1024)(128)(4,1)S(1)}, s32[]{:S(2)}) async-start(s8[9437184]{0:T(1024)(128)(4,1)} %bitcast.110), calls=%async_computation.6 | async-start | bytes 8388608
  268.0 7.5 %slice-start.2 = ((s8[9437184]{0:T(1024)(128)(4,1)}), s8[1048576]{0:T(1024)(128)(4,1)S(1)}, s32[]{:S(2)}) async-start(s8[9437184]{0:T(1024)(128)(4,1)} %bitcast.110), calls=%async_computation.7 | async-start | bytes 2097152
  291.2 33.2 %all-to-all-start.1 = ((bf16[4,576,128]{2,0,1:T(4,128)(2,1)}), bf16[4,576,128]{2,0,1:T(4,128)(2,1)S(1)}, u32[]{:S(2)}, u32[]{:S(2)}) async-start(bf16[4,576,128]{2,0,1:T(4,128)(2,1)} %copy.29), calls=%async_computation.1 | async-start | bytes 1179648 | tf_op jit(solution)/shard_map/all_to_all | solution.py:86
  305.3 112.1 %reduce-scatter.2.cloned.1.call-start = ((), (), s32[]{:S(2)}) async-start(), calls=%async_computation.4 | async-start | bytes 11796480 | tf_op jit(solution)/shard_map/reduce_scatter | solution.py:90
Sparse Core Ops, SparseCore 0:
  10.0 197.1 all-gather.1
  329.0 88.3 reduce-scatter.1
where the time goes:
time: 428 us; the launch traced here: 427 us
  waiting for transfers between devices  286 us (67%)
  matrix products  52.4 us (12%)
  local copies, waits for them, and re-layouts  36.3 us (8%)
  starting transfers between devices  27.5 us (6%)
  between operations  13.6 us (3%)
  other arithmetic  11.5 us (3%)
    all_gather x1, waiting for transfers between devices, shards(): coef_rows = lax.all_gather(coeffs, 'pair', axis=0, tiled=True)  177 us
    reduce_scatter x1, waiting for transfers between devices, shards(): lax.psum_scatter(jnp.einsum('pq,pin->qin', slab_metric, regrouped, prefer...  88.5 us
    unnamed x16, local copies, waits for them, and re-layouts  24.3 us
    all_to_all x1, waiting for transfers between devices, shards(): lax.all_to_all(half_done, 'pair', split_axis=1, concat_axis=2, tiled=True)  19 us
    dot_general x1, matrix products, shards(): jnp.einsum('ksi,gkprs->pigr', coef_piece, crossed, preferred_element_type...  15.6 us
    dot_general x1, matrix products, shards(): jnp.einsum('ksi,kgprs->pigr', coef_piece, own_mirror, preferred_element_t...  14.4 us
    all_to_all x1, starting transfers between devices, shards(): lax.all_to_all(half_done, 'pair', split_axis=1, concat_axis=2, tiled=True)  14.2 us
    all_to_all x1, starting transfers between devices, receive_rows(): lax.all_to_all(ao_blocks, 'pair', split_axis=0, concat_axis=1, tiled=True)  13.3 us
  transfers between devices with their start and end apart: 4, of which 3 were waited for; matrix products, arithmetic and copies ran while one was open for 13% of the time, Pallas kernels for 0%

commit v1 on v0

--- a/solution.py
+++ b/solution.py
@@ -5,11 +5,9 @@
 
 
 def receive_rows(ao_blocks, tile_ids, columns, half_size):
-    received = lax.all_to_all(ao_blocks, "pair", split_axis=0, concat_axis=1, tiled=True)
-    source_upper = (tile_ids[None, :] > columns[:, None])[:, :, None, None, None]
-    return jnp.where(
-        source_upper, received[:, :, :, half_size:, :], received[:, :, :, :half_size, :]
-    )
+    later = (tile_ids[:, None] > columns[None, :])[:, :, None, None, None]
+    needed = jnp.where(later, ao_blocks[:, :, :, :half_size], ao_blocks[:, :, :, half_size:])
+    return lax.all_to_all(needed, "pair", split_axis=0, concat_axis=1, tiled=True)
 
 
 def shards(ao_blocks, block_live, tile_len, coeffs, metric_panel):
@@ -84,15 +82,12 @@
     running = partial_sum + (first + jnp.concatenate([lower_rows, padding], axis=3))
     half_done = running.astype(jnp.bfloat16).reshape(slab_count, occ_count, own_count * slot_size)
     regrouped = lax.all_to_all(half_done, "pair", split_axis=1, concat_axis=2, tiled=True)
-    slab_metric = lax.dynamic_slice_in_dim(
-        metric_panel, lax.axis_index("aux") * slab_count, slab_count, 0
+    slab = lax.all_gather(regrouped, "aux", axis=0, tiled=True)
+    panel_count = metric_panel.shape[1] // lax.axis_size("aux")
+    panel_metric = lax.dynamic_slice_in_dim(
+        metric_panel, lax.axis_index("aux") * panel_count, panel_count, 1
     )
-    fitted = lax.psum_scatter(
-        jnp.einsum("pq,pin->qin", slab_metric, regrouped, preferred_element_type=jnp.float32),
-        "aux",
-        scatter_dimension=0,
-        tiled=True,
-    )
+    fitted = jnp.einsum("pq,pin->qin", panel_metric, slab, preferred_element_type=jnp.float32)
     return fitted.astype(jnp.bfloat16)
 
 

time: 428 us -> 314 us (0.73)
  waiting for transfers between devices: 286 us -> 170 us
  blocking collectives: 0 us -> 25.4 us
  starting transfers between devices: 27.5 us -> 13.3 us
  matrix products: 52.4 us -> 40.1 us
    reduce_scatter x1 -> x0, waiting for transfers between devices: 88.5 us -> none  [shards(): lax.psum_scatter(jnp.einsum('pq,pin->qin', slab_metric, regrouped, prefer...]
    all_gather x1, waiting for transfers between devices: 177 us -> 122 us  [shards(): coef_rows = lax.all_gather(coeffs, 'pair', axis=0, tiled=True)]
    all_gather x0 -> x1, waiting for transfers between devices: none -> 47.3 us  [shards(): slab = lax.all_gather(regrouped, 'aux', axis=0, tiled=True)]
    all_to_all x0 -> x1, blocking collectives: none -> 25.4 us  [shards(): lax.all_to_all(half_done, 'pair', split_axis=1, concat_axis=2, tiled=True)]
    all_to_all x2 -> x1, waiting for transfers between devices: 19 us -> 0.01 us  [receive_rows(): lax.all_to_all(needed, 'pair', split_axis=0, concat_axis=1, tiled=True)]
    all_to_all x2 -> x1, starting transfers between devices: 27.5 us -> 13.3 us  [receive_rows(): lax.all_to_all(needed, 'pair', split_axis=0, concat_axis=1, tiled=True)]
    dot_general x1, matrix products: 15.6 us -> 9.08 us  [shards(): jnp.einsum('ksi,gkprs->pigr', coef_piece, crossed, preferred_element_type...]
    select_n x0 -> x1, other arithmetic: none -> 5.11 us  [receive_rows(): jnp.where(later, ao_blocks[:, :, :, :half_size], ao_blocks[:, :, :, half_...]
  transfers between devices with their start and end apart: 4 -> 3, of which waited for: 3 -> 2; matrix products, arithmetic and copies ran while one was open for 13% -> 19% of each run, Pallas kernels for 0% -> 0%
where the time goes in v1:
time: 314 us; the launch traced here: 313 us
  waiting for transfers between devices  170 us (54%)
  matrix products  40.1 us (13%)
  local copies, waits for them, and re-layouts  36.9 us (12%)
  blocking collectives  25.4 us (8%)
  other arithmetic  14 us (4%)
  between operations  13.6 us (4%)
  starting transfers between devices  13.3 us (4%)
    all_gather x1, waiting for transfers between devices, shards(): coef_rows = lax.all_gather(coeffs, 'pair', axis=0, tiled=True)  122 us
    all_gather x1, waiting for transfers between devices, shards(): slab = lax.all_gather(regrouped, 'aux', axis=0, tiled=True)  47.3 us
    all_to_all x1, blocking collectives, shards(): lax.all_to_all(half_done, 'pair', split_axis=1, concat_axis=2, tiled=True)  25.4 us
    unnamed x12, local copies, waits for them, and re-layouts  24.3 us
    all_to_all x1, starting transfers between devices, receive_rows(): lax.all_to_all(needed, 'pair', split_axis=0, concat_axis=1, tiled=True)  13.3 us
    dot_general x1, matrix products, shards(): jnp.einsum('kri,kgprs->pigs', coef_piece, own_stored, preferred_element_t...  10.4 us
    slice x1, local copies, waits for them, and re-layouts, shards(): coef_piece[:, half_size:, :]  10.4 us
    dot_general x1, matrix products, shards(): jnp.einsum('ksi,kgprs->pigr', coef_piece, own_mirror, preferred_element_t...  9.79 us
  transfers between devices with their start and end apart: 3, of which 2 were waited for; matrix products, arithmetic and copies ran while one was open for 19% of the time, Pallas kernels for 0%

profile of v1, /device:TPU:1, one launch (start us, length us, event | category | flops | bytes accessed | tf_op | source)
XLA Modules:
  0.0 313.3 jit_solution(11316017230414143420)
XLA Ops:
  6.5 0.0 copy-start
  6.5 0.0 all-gather.3.cloned.1.call-start
  6.5 0.7 all-gather.3.cloned.1.call-update
  7.3 5.1 %slice_select_fusion = bf16[64,1,4,64,128]{4,3,2,1,0:T(8,128)(2,1)} fusion(bf16[64,1,4,128,128]{4,3,2,1,0:T(8,128)(2,1)} %param.5, pred[64]{0:T(512)(128)(4,1)S(1)} %iota_compare_fusion.8), kind=kLoop, calls=%fused_computation.18 | loop fusion | flops 2097152 | bytes 12582976 | tf_op jit(solution)/shard_map/jit(_where)/select_n | solution.py:9
  12.4 13.3 %all-to-all-start = ((bf16[64,1,4,64,128]{4,3,2,1,0:T(8,128)(2,1)}), bf16[64,1,4,64,128]{4,3,2,1,0:T(8,128)(2,1)}, u32[]{:S(2)}, u32[]{:S(2)}) async-start(bf16[64,1,4,64,128]{4,3,2,1,0:T(8,128)(2,1)} %slice_select_fusion), calls=%async_computation | async-start | bytes 8388608 | tf_op jit(solution)/shard_map/all_to_all | solution.py:10
  25.7 0.0 all-gather.5.cloned.1.call-start
  25.8 0.0 copy-done.3
  25.8 0.1 iota_compare_fusion.2
  25.8 0.1 slice.21
  26.0 0.2 dynamic-slice_reduce_fusion
  26.3 0.1 and_or_fusion
  26.4 2.5 and_bitcast_fusion
  28.9 1.3 and_bitcast_fusion.1
  30.2 4.9 %and_and_fusion = (pred[64,128,128]{2,1,0:T(8,128)(4,1)S(1)}, pred[64,128,128]{2,1,0:T(8,128)(4,1)S(1)}) fusion(pred[128]{0:T(512)(128)(4,1)S(1)} %dynamic-slice_bitcast_fusion.1, pred[64]{0:T(512)(128)(4,1)S(1)} %get-tuple-element.10, pred[64]{0:T(512)(128)(4,1)S(1)} %dynamic-slice_bitcast_fusion, pred[64,128]{1,0:T(8,128)(4,1)S(1)} %get-tuple-element.7, ...), kind=kLoop, calls=%fused_computation.23 | loop fusion | flops 12582912 | bytes 2155008 | tf_op jit(solution)/shard_map/and | solution.py:54
  35.1 121.8 %all-gather.3.cloned.1.call-done = bf16[8192,576]{0,1:T(8,128)(2,1)} async-done(((bf16[128,576]{0,1:T(8,128)(2,1)}), bf16[8192,576]{0,1:T(8,128)(2,1)}) %all-gather.3.cloned.1.call-update) | async-done | bytes 9437200 | tf_op jit(solution)/shard_map/all_gather | solution.py:66
  156.9 10.4 %copy.60 = bf16[72,8,64,128]{3,2,1,0:T(8,128)(2,1)} copy(bf16[72,8,64,128]{3,1,2,0:T(8,128)(2,1)} %bitcast.109) | data formatting | bytes 18874368
  167.3 10.4 %slice.22 = bf16[64,64,576]{1,0,2:T(8,128)(2,1)} slice(bf16[64,128,576]{1,0,2:T(8,128)(2,1)} %bitcast.105), slice={[0:64], [64:128], [0:576]} | slice | bytes 9437184 | tf_op jit(solution)/shard_map/slice | solution.py:76
  177.7 13.8 %copy.59 = bf16[64,64,576]{2,1,0:T(8,128)(2,1)} copy(bf16[64,64,576]{1,0,2:T(8,128)(2,1)} %slice.22) | data formatting | bytes 9437184
  191.6 10.4 %fusion.36 = f32[4,128,576]{1,2,0:T(8,128)} fusion(bf16[64,1,4,128,128]{4,3,2,1,0:T(8,128)(2,1)} %param.5, pred[64,128,128]{2,1,0:T(8,128)(4,1)S(1)} %get-tuple-element.6, bf16[64,128,576,1]{1,0,2,3:T(8,128)(2,1)} %bitcast.106), kind=kOutput, calls=%fused_computation.33 | convolution fusion | flops 4836032512 | bytes 20054016 | tf_op jit(solution)/shard_map/kri,kgprs->pigs/dot_general | solution.py:69
  202.0 0.0 all-to-all-done
  202.0 9.1 %fusion.31 = f32[4,576,1,64]{3,1,0,2:T(8,128)S(1)} fusion(bf16[64,128,576,1]{1,0,2,3:T(8,128)(2,1)} %bitcast.107, bf16[64,1,4,64,128]{4,3,2,1,0:T(8,128)(2,1)} %all-to-all-done, pred[64,64,128]{2,1,0:T(8,128)(4,1)S(1)} %and_bitcast_fusion), kind=kOutput, calls=%fused_computation.32 | convolution fusion | flops 2418016256 | bytes 14745600 | tf_op jit(solution)/shard_map/ksi,gkprs->pigr/dot_general | solution.py:78
  211.1 0.0 copy-done.1
  211.1 0.0 copy-start.4
  211.1 5.0 %fusion.56 = f32[4,576,1,128]{3,1,0,2:T(8,128)S(1)} fusion(bf16[64,64,576]{2,1,0:T(8,128)(2,1)S(1)} %copy-done.1, bf16[64,1,4,64,128]{4,3,2,1,0:T(8,128)(2,1)} %all-to-all-done, pred[64,64,128]{2,1,0:T(8,128)(4,1)S(1)} %and_bitcast_fusion.1, f32[4,576,1,64]{3,1,0,2:T(8,128)S(1)} %fusion.31), kind=kOutput, calls=%fused_computation.37 | convolution fusion | flops 2418311168 | bytes 11206656 | tf_op jit(solution)/shard_map/kri,gkprs->pigs/dot_general | solution.py:75
  216.1 9.8 %fusion.64 = bf16[4,576,128]{2,1,0:T(8,128)(2,1)S(1)} fusion(f32[4,576,1,128]{3,1,0,2:T(8,128)S(1)} %fusion.56, f32[4,128,576]{1,2,0:T(8,128)S(1)} %copy-done.4, bf16[64,128,576,1]{1,0,2,3:T(8,128)(2,1)} %bitcast.108, bf16[64,1,4,128,128]{4,3,2,1,0:T(8,128)(2,1)} %param.5, pred[64,128,128]{2,1,0:T(8,128)(4,1)S(1)} %get-tuple-element.5), kind=kOutput, calls=%fused_computation.39 | convolution fusion | flops 4836917248 | bytes 21823488 | tf_op jit(solution)/shard_map/ksi,kgprs->pigr/dot_general | solution.py:72
  225.9 0.5 copy.40
  226.4 25.4 %all_to_all.30 = bf16[4,576,128]{2,0,1:T(4,128)(2,1)S(1)} all-to-all(bf16[4,576,128]{2,0,1:T(4,128)(2,1)S(1)} %copy.40), channel_id=1, replica_groups=mesh['pair'=64,'aux'=4] {'pair'}, dimensions={1} | all-to-all | bytes 1179648 | tf_op jit(solution)/shard_map/all_to_all | solution.py:84
  251.8 0.1 copy.56
  252.0 1.3 reshape.328
  253.2 0.0 all-gather.5.cloned.1.call-update
  253.3 47.3 %all-gather.5.cloned.1.call-done = bf16[16,9,8192]{2,1,0:T(8,128)(2,1)} async-done(((bf16[4,9,8192]{2,1,0:T(8,128)(2,1)}), bf16[16,9,8192]{2,1,0:T(8,128)(2,1)}) %all-gather.5.cloned.1.call-update) | async-done | bytes 2359312 | tf_op jit(solution)/shard_map/all_gather | solution.py:85
  300.6 5.8 %convolution_convert_fusion = bf16[8,9,8192]{2,0,1:T(8,128)(2,1)} fusion(bf16[16,9,8192]{2,1,0:T(8,128)(2,1)} %all-gather.5.cloned.1.call-done, bf16[16,32]{1,0:T(8,128)(2,1)S(1)} %copy-done, s32[]{:T(128)S(6)} %select_n.35), kind=kOutput, calls=%fused_computation | convolution fusion | flops 19464192 | bytes 3539972 | tf_op jit(solution)/shard_map/pq,pin->qin/dot_general | solution.py:90
  (16 shorter events, 0.1 us)
Async XLA Ops:
  6.5 294.1 %copy-start = (bf16[16,32]{1,0:T(8,128)(2,1)S(1)}, bf16[16,32]{1,0:T(8,128)(2,1)}, u32[]{:S(2)}) copy-start(bf16[16,32]{1,0:T(8,128)(2,1)} %param.9) | copy-start | bytes 3076
  6.5 150.3 %all-gather.3.cloned.1.call-start = ((), (), s32[]{:S(2)}) async-start(), calls=%async_computation.2 | async-start | bytes 9584640 | tf_op jit(solution)/shard_map/all_gather | solution.py:66
  12.4 13.4 %copy-start.3 = (s32[64]{0:T(128)S(1)}, s32[64]{0:T(128)}, u32[]{:S(2)}) copy-start(s32[64]{0:T(128)} %param.7) | copy-start | bytes 772
  12.4 13.6 %copy-start.2 = (s32[64,64]{1,0:T(8,128)S(1)}, s32[64,64]{1,0:T(8,128)}, u32[]{:S(2)}) copy-start(s32[64,64]{1,0:T(8,128)} %param.6) | copy-start | bytes 49156
  12.4 189.6 %all-to-all-start = ((bf16[64,1,4,64,128]{4,3,2,1,0:T(8,128)(2,1)}), bf16[64,1,4,64,128]{4,3,2,1,0:T(8,128)(2,1)}, u32[]{:S(2)}, u32[]{:S(2)}) async-start(bf16[64,1,4,64,128]{4,3,2,1,0:T(8,128)(2,1)} %slice_select_fusion), calls=%async_computation | async-start | bytes 8388608 | tf_op jit(solution)/shard_map/all_to_all | solution.py:10
  25.7 274.9 %all-gather.5.cloned.1.call-start = ((), (), s32[]{:S(2)}) async-start(), calls=%async_computation.3 | async-start | bytes 5242880 | tf_op jit(solution)/shard_map/all_gather | solution.py:85
  202.0 9.1 %copy-start.1 = (bf16[64,64,576]{2,1,0:T(8,128)(2,1)S(1)}, bf16[64,64,576]{2,1,0:T(8,128)(2,1)}, u32[]{:S(2)}) copy-start(bf16[64,64,576]{2,1,0:T(8,128)(2,1)} %copy.59) | copy-start | bytes 14155780
  211.1 5.0 %copy-start.4 = (f32[4,128,576]{1,2,0:T(8,128)S(1)}, f32[4,128,576]{1,2,0:T(8,128)}, u32[]{:S(2)}) copy-start(f32[4,128,576]{1,2,0:T(8,128)} %fusion.36) | copy-start | bytes 3538948
Sparse Core Ops, SparseCore 0:
  10.0 146.8 all-gather.2
  253.4 47.1 all-gather.4

commit v2 on v1

v2 whole, which is shorter than its diff:
```python
import functools

import jax
import jax.numpy as jnp
from jax import lax
from jax.experimental import pallas as pl
from jax.experimental.pallas import tpu as pltpu
from jax.sharding import PartitionSpec as P

MESH = pl.DeviceIdType.MESH
PLANES = 8
REACH = 4
F32 = jnp.float32
BF16 = jnp.bfloat16


def exchange_kernel(peers, ao, got, send_sem, recv_sem, own_sem):
    me, aux = lax.axis_index("pair"), lax.axis_index("aux")
    plane, slot = me // peers, me % peers
    half = ao.shape[3] // 2

    def piece(tile):
        start = pl.multiple_of(jnp.where(tile > me, 0, half), half)
        return ao.at[tile, 0, :, pl.ds(start, half), :]

    def send(group, step):
        other = lax.rem(slot + step, peers)
        return pltpu.make_async_remote_copy(
            src_ref=piece(group * peers + other),
            dst_ref=got.at[group, slot],
            send_sem=send_sem.at[group, step],
            recv_sem=recv_sem.at[group, step],
            device_id=(plane * peers + other, aux),
            device_id_type=MESH,
        )

    def keep(group):
        return pltpu.make_async_copy(
            piece(group * peers + slot), got.at[group, slot], own_sem.at[group]
        )

    barrier = pltpu.get_barrier_semaphore()
    for step in range(1, peers):
        other = lax.rem(slot + step, peers)
        pl.semaphore_signal(
            barrier, inc=1, device_id=(plane * peers + other, aux), device_id_type=MESH
        )
    pl.semaphore_wait(barrier, peers - 1)

    @pl.loop(0, PLANES)
    def _(group):
        keep(group).start()
        for step in range(1, peers):
            send(group, step).start()

    @pl.loop(0, PLANES)
    def _(group):
        keep(group).wait()
        for step in range(1, peers):
            send(group, step).wait()


def exchange(ao, peers):
    tiles, _, slab, size, width = ao.shape
    return pl.pallas_call(
        functools.partial(exchange_kernel, peers),
        out_shape=jax.ShapeDtypeStruct((PLANES, peers, slab, size // 2, width), ao.dtype),
        in_specs=[pl.BlockSpec(memory_space=pl.ANY)],
        out_specs=pl.BlockSpec(memory_space=pl.ANY),
        scratch_shapes=[
            pltpu.SemaphoreType.DMA((PLANES, peers)),
            pltpu.SemaphoreType.DMA((PLANES, peers)),
            pltpu.SemaphoreType.DMA((PLANES,)),
        ],
        compiler_params=pltpu.CompilerParams(collective_id=0, has_side_effects=True),
        cost_estimate=pl.CostEstimate(flops=0, bytes_accessed=180_000_000, transcendentals=0),
    )(ao)


def partial_kernel(peers, place, live, coef_group, coef_plane, ao, got, out, direct, mirror):
    plane, me = place[0], place[1]
    step = pl.program_id(0)
    group = lax.rem(plane + 1 + step, PLANES)
    slab, size = ao.shape[2], ao.shape[3]
    half = size // 2
    target = group * peers + lax.rem(me, peers)
    row = lax.broadcasted_iota(jnp.int32, (size, size), 0)
    col = lax.broadcasted_iota(jnp.int32, (size, size), 1)

    def one(cond):
        return jnp.where(cond, 1.0, 0.0).astype(F32)

    def kept(first, second):
        return one(live[jnp.maximum(first, second), jnp.minimum(first, second)] > 0)

    def wide(ref):
        return jnp.concatenate([ref[m] for m in range(peers)], axis=1)

    def straight(left, right):
        return lax.dot_general(left, right, (((1,), (0,)), ((), ())), preferred_element_type=F32)

    def turned(left, right):
        return lax.dot_general(left, right, (((1,), (1,)), ((), ())), preferred_element_type=F32)

    @pl.when(step == 0)
    def _():
        direct[...] = jnp.zeros_like(direct)

    mirror[...] = jnp.zeros_like(mirror)

    @pl.when(group >= plane)
    def _():
        blocks = []
        for m in range(peers):
            tile = group * peers + m
            use = kept(tile, me)
            mask = use * (
                one(tile > me) * one(row < half) + one(tile == me) * one(row >= col)
            )
            mask = mask.astype(BF16)
            blocks.append(jnp.concatenate([ao[m, 0, p] * mask for p in range(slab)], axis=1))
        direct[...] += straight(wide(coef_group), jnp.concatenate(blocks, axis=0))
        blocks = []
        for m in range(peers):
            tile = plane * peers + m
            use = kept(tile, target) * one(tile < target)
            mask = jnp.full((half, size), use, F32).astype(BF16)
            zero = jnp.zeros((half, size), BF16)
            rows = []
            for p in range(slab):
                rows += [got[0, m, p] * mask, zero]
            blocks.append(jnp.concatenate(rows, axis=0))
        mirror[...] += turned(wide(coef_plane), jnp.concatenate(blocks, axis=1))

    @pl.when(group <= plane)
    def _():
        blocks = []
        for m in range(peers):
            tile = group * peers + m
            use = kept(tile, me)
            mask = use * (
                one(tile < me) * one(row >= half) + one(tile == me) * one(row > col)
            )
            mask = mask.astype(BF16)
            blocks.append(jnp.concatenate([ao[m, 0, p] * mask for p in range(slab)], axis=0))
        direct[...] += turned(wide(coef_group), jnp.concatenate(blocks, axis=1))
        blocks = []
        for m in range(peers):
            tile = plane * peers + m
            use = kept(tile, target) * one(tile > target)
            mask = jnp.full((half, size), use, F32).astype(BF16)
            zero = jnp.zeros((half, size), BF16)
            blocks.append(zero)
            blocks[-1] = jnp.concatenate(
                [jnp.concatenate([zero, got[0, m, p] * mask], axis=0) for p in range(slab)], axis=1
            )
        mirror[...] += straight(wide(coef_plane), jnp.concatenate(blocks, axis=0))

    @pl.when(step == PLANES - 1)
    def _():
        mirror[...] += direct[...]

    chunk = mirror.shape[0] // PLANES
    for z in range(PLANES):
        for p in range(slab):
            out[0, z, p // 2, (p % 2) * chunk : (p % 2 + 1) * chunk, :] = mirror[
                z * chunk : (z + 1) * chunk, p * size : (p + 1) * size
            ]


def partials(ao, got, coefs, block_live, peers):
    _, _, slab, size, _ = ao.shape
    occ = coefs.shape[1]
    me = lax.axis_index("pair")
    place = jnp.stack([me // peers, me]).astype(jnp.int32)

    def at_group(step, place, live):
        return lax.rem(place[0] + 1 + step, PLANES)

    rows = 2 * occ // PLANES
    spec = pltpu.PrefetchScalarGridSpec(
        num_scalar_prefetch=2,
        grid=(PLANES,),
        in_specs=[
            pl.BlockSpec((peers, occ, size), lambda s, p, l: (at_group(s, p, l), 0, 0)),
            pl.BlockSpec((peers, occ, size), lambda s, p, l: (p[0], 0, 0)),
            pl.BlockSpec(
                (peers, 1, slab, size, size), lambda s, p, l: (at_group(s, p, l), 0, 0, 0, 0)
            ),
            pl.BlockSpec(
                (1, peers, slab, size // 2, size), lambda s, p, l: (at_group(s, p, l), 0, 0, 0, 0)
            ),
        ],
        out_specs=pl.BlockSpec(
            (1, PLANES, 2, rows, size), lambda s, p, l: (at_group(s, p, l), 0, 0, 0, 0)
        ),
        scratch_shapes=[pltpu.VMEM((occ, slab * size), F32), pltpu.VMEM((occ, slab * size), F32)],
    )
    return pl.pallas_call(
        functools.partial(partial_kernel, peers),
        grid_spec=spec,
        out_shape=jax.ShapeDtypeStruct((PLANES, PLANES, 2, rows, size), F32),
        compiler_params=pltpu.CompilerParams(vmem_limit_bytes=48 << 20),
    )(place, block_live, coefs, coefs, ao, got)


def ring_kernel(
    peers, ranks, parts, out, own, own_sem, sent, came, send_sem, recv_sem, total, padded, sheet, seen,
    plane_send, plane_recv, line_send, line_recv, line_own,
):
    me, aux = lax.axis_index("pair"), lax.axis_index("aux")
    plane, slot = me // peers, me % peers
    share = parts.shape[3] // (2 * peers)

    def shifted(move):
        return lax.rem(plane + move + PLANES, PLANES)

    def load(group):
        return pltpu.make_async_copy(parts.at[group], own.at[group], own_sem.at[group])

    def hop(way, group, left):
        halves = pl.ds(way, 1) if left == REACH else pl.ds(0, 2)
        return pltpu.make_async_remote_copy(
            src_ref=sent.at[way, group, left - 1, halves],
            dst_ref=came.at[way, group, left - 1, halves],
            send_sem=send_sem.at[way, group, left - 1],
            recv_sem=recv_sem.at[way, group, left - 1],
            device_id=(shifted(1 if way == 0 else -1) * peers + slot, aux),
            device_id_type=MESH,
        )

    def spread(group, step):
        other = lax.rem(slot + step, peers)
        return pltpu.make_async_remote_copy(
            src_ref=sheet.at[group, other],
            dst_ref=seen.at[group, slot],
            send_sem=plane_send.at[group, step],
            recv_sem=plane_recv.at[group, step],
            device_id=(plane * peers + other, aux),
            device_id_type=MESH,
        )

    def line(group, step):
        return pltpu.make_async_remote_copy(
            src_ref=seen.at[group],
            dst_ref=out.at[group, aux],
            send_sem=line_send.at[group, step],
            recv_sem=line_recv.at[group, step],
            device_id=(me, lax.rem(aux + step, ranks)),
            device_id_type=MESH,
        )

    def line_keep(group):
        return pltpu.make_async_copy(seen.at[group], out.at[group, aux], line_own.at[group])

    barrier = pltpu.get_barrier_semaphore()
    for move in (1, -1):
        pl.semaphore_signal(
            barrier, inc=1, device_id=(shifted(move) * peers + slot, aux), device_id_type=MESH
        )
    for step in range(1, peers):
        pl.semaphore_signal(
            barrier,
            inc=1,
            device_id=(plane * peers + lax.rem(slot + step, peers), aux),
            device_id_type=MESH,
        )
    for step in range(1, ranks):
        pl.semaphore_signal(
            barrier, inc=1, device_id=(me, lax.rem(aux + step, ranks)), device_id_type=MESH
        )

    @pl.loop(0, PLANES)
    def _(group):
        load(group).start()

    padded[...] = jnp.zeros_like(padded)
    pl.semaphore_wait(barrier, 2 + peers - 1 + ranks - 1)

    def pass_on(group, left):
        for way in range(2):
            goal = shifted(left if way == 0 else -left)
            if left == REACH:
                sent[way, group, left - 1, way] = own[group, goal, way].astype(BF16)
            else:
                hop(way, group, left + 1).wait_recv()
                for half in range(2):
                    value = own[group, goal, half]
                    if left < REACH - 1 or half == way:
                        value = value + came[way, group, left, half].astype(F32)
                    sent[way, group, left - 1, half] = value.astype(BF16)
            hop(way, group, left).start()

    def finish(group):
        for way in range(2):
            hop(way, group, 1).wait_recv()
        for half in range(2):
            total[half] = (
                own[group, plane, half]
                + came[0, group, 0, half].astype(F32)
                + came[1, group, 0, half].astype(F32)
            )
        for other in range(peers):
            for half in range(2):
                for odd in range(2):
                    start = odd * peers * share + other * share
                    place = (half * 2 + odd) * share
                    padded[other, place : place + share, :] = total[half, start : start + share, :]
            sheet[group, other] = padded[other].astype(BF16)
        seen[group, slot] = sheet[group, slot]
        for step in range(1, peers):
            spread(group, step).start()

    def along(group):
        for step in range(1, peers):
            spread(group, step).wait_recv()
        line_keep(group).start()
        for step in range(1, ranks):
            line(group, step).start()

    @pl.loop(0, PLANES + REACH + 1)
    def _(turn):
        @pl.when(turn < PLANES)
        def _():
            load(turn).wait()
            pass_on(turn, REACH)

        for left in range(REACH - 1, 0, -1):
            group = turn - (REACH - left)

            @pl.when((group >= 0) & (group < PLANES))
            def _(group=group, left=left):
                pass_on(group, left)

        group = turn - REACH

        @pl.when((group >= 0) & (group < PLANES))
        def _(group=group):
            finish(group)

        group = turn - REACH - 1

        @pl.when((group >= 0) & (group < PLANES))
        def _(group=group):
            along(group)

    @pl.loop(0, PLANES)
    def _(group):
        line_keep(group).wait()
        for step in range(1, ranks):
            line(group, step).wait()
        for step in range(1, peers):
            spread(group, step).wait_send()
        for way in range(2):
            for left in range(1, REACH + 1):
                hop(way, group, left).wait_send()


def ring(parts, peers, ranks):
    _, _, _, rows, size = parts.shape
    need = 2 * rows // peers
    room = -(-need // 16) * 16
    return pl.pallas_call(
        functools.partial(ring_kernel, peers, ranks),
        out_shape=jax.ShapeDtypeStruct((PLANES, ranks, peers, room, size), BF16),
        in_specs=[pl.BlockSpec(memory_space=pl.ANY)],
        out_specs=pl.BlockSpec(memory_space=pl.ANY),
        scratch_shapes=[
            pltpu.VMEM(parts.shape, F32),
            pltpu.SemaphoreType.DMA((PLANES,)),
            pltpu.VMEM((2, PLANES, REACH, 2, rows, size), BF16),
            pltpu.VMEM((2, PLANES, REACH, 2, rows, size), BF16),
            pltpu.SemaphoreType.DMA((2, PLANES, REACH)),
            pltpu.SemaphoreType.DMA((2, PLANES, REACH)),
            pltpu.VMEM((2, rows, size), F32),
            pltpu.VMEM((peers, room, size), F32),
            pltpu.VMEM((PLANES, peers, room, size), BF16),
            pltpu.VMEM((PLANES, peers, room, size), BF16),
            pltpu.SemaphoreType.DMA((PLANES, peers)),
            pltpu.SemaphoreType.DMA((PLANES, peers)),
            pltpu.SemaphoreType.DMA((PLANES, ranks)),
            pltpu.SemaphoreType.DMA((PLANES, ranks)),
            pltpu.SemaphoreType.DMA((PLANES,)),
        ],
        compiler_params=pltpu.CompilerParams(
            collective_id=1, has_side_effects=True, vmem_limit_bytes=48 << 20
        ),
        cost_estimate=pl.CostEstimate(flops=0, bytes_accessed=180_000_000, transcendentals=0),
    )(parts)


def fit_kernel(peers, lengths, weights, slabs, out):
    group = pl.program_id(0)
    ranks, _, room, size = slabs.shape[1:]
    panel, share = out.shape[0], out.shape[1]
    inside = lax.broadcasted_iota(jnp.int32, (1, size), 1)
    blocks = [
        jnp.concatenate([slabs[0, r, m] for r in range(ranks)], axis=0) for m in range(peers)
    ]
    result = jnp.dot(
        weights[...], jnp.concatenate(blocks, axis=1), preferred_element_type=F32
    )
    for m in range(peers):
        valid = jnp.broadcast_to(inside < lengths[group * peers + m], (share, size))
        for q in range(panel):
            value = result[16 * q : 16 * q + share, m * size : (m + 1) * size]
            out[q, :, m * size : (m + 1) * size] = jnp.where(valid, value, 0.0).astype(BF16)


def fit(slabs, metric, tile_len, share):
    groups, ranks, peers, room, size = slabs.shape
    slab, panel_all = metric.shape
    panel = panel_all // ranks
    local = lax.dynamic_slice_in_dim(metric, lax.axis_index("aux") * panel, panel, 1)
    weights = jnp.einsum(
        "pq,ij->qipj", local.astype(F32), jnp.eye(16, share, dtype=F32)
    ).reshape(panel * 16, ranks, slab // ranks * share)
    weights = jnp.pad(weights, ((0, 0), (0, 0), (0, room - weights.shape[2])))
    weights = weights.reshape(panel * 16, ranks * room).astype(BF16)
    spec = pltpu.PrefetchScalarGridSpec(
        num_scalar_prefetch=1,
        grid=(groups,),
        in_specs=[
            pl.BlockSpec(weights.shape, lambda g, l: (0, 0)),
            pl.BlockSpec((1, ranks, peers, room, size), lambda g, l: (g, 0, 0, 0, 0)),
        ],
        out_specs=pl.BlockSpec((panel, share, peers * size), lambda g, l: (0, 0, g)),
    )
    return pl.pallas_call(
        functools.partial(fit_kernel, peers),
        grid_spec=spec,
        out_shape=jax.ShapeDtypeStruct((panel, share, groups * peers * size), BF16),
        compiler_params=pltpu.CompilerParams(vmem_limit_bytes=32 << 20),
    )(tile_len, weights, slabs)


def shards(ao_blocks, block_live, tile_len, coeffs, metric_panel):
    pairs, ranks = lax.axis_size("pair"), lax.axis_size("aux")
    peers = pairs // PLANES
    me, aux = lax.axis_index("pair"), lax.axis_index("aux")
    size, occ = coeffs.shape
    inside = jnp.arange(size, dtype=jnp.int32)
    valid = inside < lax.dynamic_index_in_dim(tile_len, me, 0, keepdims=False)
    turned = jnp.where(valid[None, :], jnp.transpose(coeffs), jnp.zeros((), coeffs.dtype))
    part = lax.dynamic_slice_in_dim(turned, aux * (occ // ranks), occ // ranks, 0)
    coefs = lax.all_gather(part[None], ("pair", "aux"), axis=0, tiled=True)
    coefs = coefs.reshape(pairs, occ, size)
    got = exchange(ao_blocks, peers)
    parts = partials(ao_blocks, got, coefs, block_live, peers)
    slabs = ring(parts, peers, ranks)
    return fit(slabs, metric_panel, tile_len, occ // pairs)


def solution(mesh):
    in_specs = (P(None, "pair", "aux", None, None), P(), P(), P("pair", None), P())
    out_specs = P("aux", "pair", None)
    return jax.shard_map(shards, mesh=mesh, in_specs=in_specs, out_specs=out_specs, check_vma=False)
```

time: 314 us -> 237 us (0.75)
  Pallas kernels: 0 us -> 146 us
  waiting for transfers between devices: 170 us -> 69.7 us
  matrix products: 40.1 us -> 0 us
  local copies, waits for them, and re-layouts: 36.9 us -> 5.49 us
  blocking collectives: 25.4 us -> 0 us
  starting transfers between devices: 13.3 us -> 0.01 us
  other arithmetic: 14 us -> 2.33 us
    pallas_call x0 -> x4, Pallas kernels: none -> 146 us  [the longest x1 68.9 us: ring(): pl.pallas_call(functools.partial(ring_kernel, peers, ranks), out_shape=ja...]
    all_gather x2 -> x1, waiting for transfers between devices: 169 us -> 69.7 us  [shards(): coefs = lax.all_gather(part[None], ('pair', 'aux'), axis=0, tiled=True)]
    dot_general x5 -> x0, matrix products: 40.1 us -> none  [the longest x1 10.4 us: shards(): jnp.einsum('kri,kgprs->pigs', coef_piece, own_stored, preferred_element_t...]
    all_to_all x1 -> x0, blocking collectives: 25.4 us -> none  [shards(): lax.all_to_all(half_done, 'pair', split_axis=1, concat_axis=2, tiled=True)]
    unnamed x12 -> x8, local copies, waits for them, and re-layouts: 24.3 us -> 2.2 us
    all_to_all x1 -> x0, starting transfers between devices: 13.3 us -> none  [receive_rows(): lax.all_to_all(needed, 'pair', split_axis=0, concat_axis=1, tiled=True)]
    slice x4 -> x0, local copies, waits for them, and re-layouts: 10.5 us -> none  [the longest x1 10.4 us: shards(): coef_piece[:, half_size:, :]]
    select_n x1 -> x0, other arithmetic: 5.11 us -> none  [receive_rows(): jnp.where(later, ao_blocks[:, :, :, :half_size], ao_blocks[:, :, :, half_...]
  transfers between devices with their start and end apart: 3 -> 1, of which waited for: 2 -> 1; matrix products, arithmetic and copies ran while one was open for 19% -> 0% of each run, Pallas kernels for 0% -> 23%
where the time goes in v2:
time: 237 us
  Pallas kernels  146 us (62%)
  waiting for transfers between devices  69.7 us (29%)
  between operations  13.5 us (6%)
  local copies, waits for them, and re-layouts  5.49 us (2%)
    all_gather x1, waiting for transfers between devices, shards(): coefs = lax.all_gather(part[None], ('pair', 'aux'), axis=0, tiled=True)  69.7 us
    pallas_call x1, Pallas kernels, ring(): pl.pallas_call(functools.partial(ring_kernel, peers, ranks), out_shape=ja...  68.9 us
    pallas_call x1, Pallas kernels, exchange(): pl.pallas_call(functools.partial(exchange_kernel, peers), out_shape=jax.S...  54.4 us
    pallas_call x1, Pallas kernels, partials(): pl.pallas_call(functools.partial(partial_kernel, peers), grid_spec=spec,...  19.9 us
  transfers between devices with their start and end apart: 1, of which 1 were waited for; matrix products, arithmetic and copies ran while one was open for 0% of the time, Pallas kernels for 23%

profile of v2, /device:TPU:1, one launch (start us, length us, event | category | flops | bytes accessed | tf_op | source)
XLA Modules:
  0.0 236.7 jit_solution(828985331186064436)
XLA Ops:
  6.5 0.0 all-gather.3.cloned.1.call-start
  6.5 1.2 dynamic_slice.11
  7.8 0.6 iota_compare_fusion.1
  8.4 1.4 fusion.1
  9.8 0.0 all-gather.3.cloned.1.call-update
  9.9 0.0 copy-start.3
  9.9 0.0 copy-start.1
  9.9 54.4 %shard_map.55.got = bf16[8,8,4,64,128]{4,3,2,1,0:T(8,128)(2,1)} custom-call(bf16[64,1,4,128,128]{4,3,2,1,0:T(8,128)(2,1)} %ao.3), custom_call_target="tpu_custom_call" | custom-call | bytes 180000000 | tf_op jit(solution)/shard_map/pallas_call | solution.py:65
  64.3 0.0 copy-done.3
  64.3 0.1 dynamic-slice_convert_fusion
  64.4 0.1 fusion
  64.5 0.2 reshape.13
  64.7 0.1 copy.8.weights
  64.8 0.1 pad_add_fusion.place
  64.9 69.7 %all-gather.3.cloned.1.call-done = bf16[36864,128]{1,0:T(8,128)(2,1)} async-done(((bf16[144,128]{1,0:T(8,128)(2,1)}), bf16[36864,128]{1,0:T(8,128)(2,1)}) %all-gather.3.cloned.1.call-update) | async-done | bytes 9437200 | tf_op jit(solution)/shard_map/all_gather | solution.py:446
  134.6 0.0 copy-done.1
  134.6 0.0 copy-start
  134.6 2.2 copy-done
  136.8 19.9 %shard_map.56.parts = f32[8,8,2,144,128]{4,3,2,1,0:T(8,128)} custom-call(s32[2]{0:T(128)S(1)} %pad_add_fusion.place, s32[64,64]{1,0:T(8,128)S(1)} %copy-done.1, bf16[64,576,128]{2,1,0:T(8,128)(2,1)} %bitcast.13, bf16[64,576,128]{2,1,0:T(8,128)(2,1)} %bitcast.14, bf16[64,1,4,128,128]{4,3,2,1,0:T(8,128)(2,1)} %ao.3, bf16[8,8,4,64,128]{4,3,2,1,0:T(8,128)(2,1)S(1)} %copy-done), custom_call_target="tpu_custom_call" | custom-call | tf_op jit(solution)/shard_map/pallas_call | solution.py:199
  156.7 0.0 copy-start.2
  156.7 68.9 %shard_map.57.slabs = bf16[8,4,8,48,128]{4,3,2,1,0:T(8,128)(2,1)S(1)} custom-call(f32[8,8,2,144,128]{4,3,2,1,0:T(8,128)} %shard_map.56.parts), custom_call_target="tpu_custom_call" | custom-call | bytes 180000000 | tf_op jit(solution)/shard_map/pallas_call | solution.py:363
  225.6 0.0 copy-done.2
  225.6 2.5 %shard_map.58 = bf16[8,9,8192]{2,1,0:T(8,128)(2,1)S(1)} custom-call(s32[64]{0:T(128)S(1)} %copy-done.2, bf16[128,192]{1,0:T(8,128)(2,1)S(1)} %copy.8.weights, bf16[8,4,8,48,128]{4,3,2,1,0:T(8,128)(2,1)S(1)} %shard_map.57.slabs), custom_call_target="tpu_custom_call" | custom-call | tf_op jit(solution)/shard_map/pallas_call | solution.py:429
  228.1 1.7 copy.9
  (2 shorter events, 0.0 us)
Async XLA Ops:
  6.5 128.0 %all-gather.3.cloned.1.call-start = ((), (), s32[]{:S(2)}) async-start(), calls=%async_computation | async-start | bytes 9474048 | tf_op jit(solution)/shard_map/all_gather | solution.py:446
  9.9 54.4 %copy-start.3 = (bf16[16,32]{1,0:T(8,128)(2,1)S(1)}, bf16[16,32]{1,0:T(8,128)(2,1)}, u32[]{:S(2)}) copy-start(bf16[16,32]{1,0:T(8,128)(2,1)} %param.9) | copy-start | bytes 3076
  9.9 124.7 %copy-start.1 = (s32[64,64]{1,0:T(8,128)S(1)}, s32[64,64]{1,0:T(8,128)}, u32[]{:S(2)}) copy-start(s32[64,64]{1,0:T(8,128)} %live.1) | copy-start | bytes 49156
  134.6 2.2 copy-start
  156.7 68.9 %copy-start.2 = (s32[64]{0:T(128)S(1)}, s32[64]{0:T(128)}, u32[]{:S(2)}) copy-start(s32[64]{0:T(128)} %lengths.1) | copy-start | bytes 772
Sparse Core Ops, SparseCore 0:
  11.2 123.3 all-gather.2

commit v3 on v2

--- a/solution.py
+++ b/solution.py
@@ -14,9 +14,14 @@
 BF16 = jnp.bfloat16
 
 
-def exchange_kernel(peers, ao, got, send_sem, recv_sem, own_sem):
+def exchange_kernel(
+    peers, ranks, ao, mine, got, coefs, send_sem, recv_sem, own_sem, z_send, z_recv, x_send, x_recv,
+    y_send, y_recv, core_send, core_recv, mine_sem,
+):
     me, aux = lax.axis_index("pair"), lax.axis_index("aux")
     plane, slot = me // peers, me % peers
+    chips = peers // 2
+    chip, core = slot // 2, slot % 2
     half = ao.shape[3] // 2
 
     def piece(tile):
@@ -39,42 +44,172 @@
             piece(group * peers + slot), got.at[group, slot], own_sem.at[group]
         )
 
+    def along_z(step):
+        return pltpu.make_async_remote_copy(
+            src_ref=mine.at[aux],
+            dst_ref=coefs.at[plane, slot, aux],
+            send_sem=z_send.at[step],
+            recv_sem=z_recv.at[step],
+            device_id=(lax.rem(plane + step, PLANES) * peers + slot, aux),
+            device_id_type=MESH,
+        )
+
+    def batch(step, rank):
+        source = lax.rem(chip - step + chips, chips) * 2 + core
+        return coefs.at[:, source, rank]
+
+    def along_x(step):
+        other = lax.rem(chip + step, chips) * 2 + core
+        return pltpu.make_async_remote_copy(
+            src_ref=batch(0, aux),
+            dst_ref=batch(0, aux),
+            send_sem=x_send.at[step],
+            recv_sem=x_recv.at[step],
+            device_id=(plane * peers + other, aux),
+            device_id_type=MESH,
+        )
+
+    def along_y(step, leg):
+        way = 1 if leg == 0 or (leg == 2 and step % 2 == 0) else -1
+        rank = aux if leg < 2 else lax.rem(aux - way + ranks, ranks)
+        return pltpu.make_async_remote_copy(
+            src_ref=batch(step, rank),
+            dst_ref=batch(step, rank),
+            send_sem=y_send.at[step, leg],
+            recv_sem=y_recv.at[step, leg],
+            device_id=(me, lax.rem(aux + way + ranks, ranks)),
+            device_id_type=MESH,
+        )
+
+    def across(step, leg):
+        rank = lax.rem(aux + (0, -1, 1, 2)[leg] + ranks, ranks)
+        return pltpu.make_async_remote_copy(
+            src_ref=batch(step, rank),
+            dst_ref=batch(step, rank),
+            send_sem=core_send.at[step, leg],
+            recv_sem=core_recv.at[step, leg],
+            device_id=(me + 1 - 2 * core, aux),
+            device_id_type=MESH,
+        )
+
     barrier = pltpu.get_barrier_semaphore()
+
+    def greet(device):
+        pl.semaphore_signal(barrier, inc=1, device_id=device, device_id_type=MESH)
+
     for step in range(1, peers):
-        other = lax.rem(slot + step, peers)
-        pl.semaphore_signal(
-            barrier, inc=1, device_id=(plane * peers + other, aux), device_id_type=MESH
-        )
-    pl.semaphore_wait(barrier, peers - 1)
-
-    @pl.loop(0, PLANES)
-    def _(group):
-        keep(group).start()
-        for step in range(1, peers):
-            send(group, step).start()
+        greet((plane * peers + lax.rem(slot + step, peers), aux))
+    for step in range(1, PLANES):
+        greet((lax.rem(plane + step, PLANES) * peers + slot, aux))
+    for step in (1, ranks - 1):
+        greet((me, lax.rem(aux + step, ranks)))
+    pl.semaphore_wait(barrier, peers + PLANES)
+
+    own_part = pltpu.make_async_copy(mine.at[aux], coefs.at[plane, slot, aux], mine_sem)
+    own_part.start()
+    for step in range(1, PLANES):
+        along_z(step).start()
+
+    def offer(step):
+        across(step, 0).start()
+        along_y(step, 0).start()
+        along_y(step, 1).start()
+
+    def relay(step):
+        along_y(step, 0).wait_recv()
+        along_y(step, 1).wait_recv()
+        along_y(step, 2).start()
+        across(step, 1).start()
+        across(step, 2).start()
+
+    def close(step):
+        along_y(step, 2).wait_recv()
+        across(step, 3).start()
+
+    @pl.loop(0, max(PLANES + 1, chips + 4))
+    def _(turn):
+        @pl.when(turn < PLANES)
+        def _():
+            keep(turn).start()
+            for step in range(1, peers):
+                send(turn, step).start()
+
+        @pl.when(turn == 1)
+        def _():
+            own_part.wait()
+            for step in range(1, PLANES):
+                along_z(step).wait_recv()
+            for step in range(1, chips):
+                along_x(step).start()
+            offer(0)
+
+        @pl.when(turn == 2)
+        def _():
+            for step in range(1, chips):
+                along_x(step).wait_recv()
+                offer(step)
+
+        for step in range(chips):
+            @pl.when(turn == 3 + step)
+            def _(step=step):
+                relay(step)
+
+            @pl.when(turn == 4 + step)
+            def _(step=step):
+                close(step)
+
+        @pl.when((turn >= 2) & (turn <= PLANES))
+        def _():
+            for step in range(1, peers):
+                send(turn - 2, step).wait_send()
+
+    for step in range(1, peers):
+        send(PLANES - 1, step).wait_send()
+    for step in range(1, PLANES):
+        along_z(step).wait_send()
+    for step in range(1, chips):
+        along_x(step).wait_send()
+    for step in range(chips):
+        for leg in range(3):
+            along_y(step, leg).wait_send()
+        for leg in range(4):
+            across(step, leg).wait()
 
     @pl.loop(0, PLANES)
     def _(group):
         keep(group).wait()
         for step in range(1, peers):
-            send(group, step).wait()
-
-
-def exchange(ao, peers):
-    tiles, _, slab, size, width = ao.shape
+            send(group, step).wait_recv()
+
+
+def exchange(ao, mine, peers, ranks):
+    _, _, slab, size, width = ao.shape
+    chips = peers // 2
+    dma = pltpu.SemaphoreType.DMA
     return pl.pallas_call(
-        functools.partial(exchange_kernel, peers),
-        out_shape=jax.ShapeDtypeStruct((PLANES, peers, slab, size // 2, width), ao.dtype),
-        in_specs=[pl.BlockSpec(memory_space=pl.ANY)],
-        out_specs=pl.BlockSpec(memory_space=pl.ANY),
+        functools.partial(exchange_kernel, peers, ranks),
+        out_shape=(
+            jax.ShapeDtypeStruct((PLANES, peers, slab, size // 2, width), ao.dtype),
+            jax.ShapeDtypeStruct((PLANES, peers) + mine.shape, mine.dtype),
+        ),
+        in_specs=[pl.BlockSpec(memory_space=pl.ANY)] * 2,
+        out_specs=(pl.BlockSpec(memory_space=pl.ANY),) * 2,
         scratch_shapes=[
-            pltpu.SemaphoreType.DMA((PLANES, peers)),
-            pltpu.SemaphoreType.DMA((PLANES, peers)),
-            pltpu.SemaphoreType.DMA((PLANES,)),
+            dma((PLANES, peers)),
+            dma((PLANES, peers)),
+            dma((PLANES,)),
+            dma((PLANES,)),
+            dma((PLANES,)),
+            dma((chips,)),
+            dma((chips,)),
+            dma((chips, 3)),
+            dma((chips, 3)),
+            dma((chips, 4)),
+            dma((chips, 4)),
+            dma(()),
         ],
         compiler_params=pltpu.CompilerParams(collective_id=0, has_side_effects=True),
-        cost_estimate=pl.CostEstimate(flops=0, bytes_accessed=180_000_000, transcendentals=0),
-    )(ao)
+    )(ao, mine)
 
 
 def partial_kernel(peers, place, live, coef_group, coef_plane, ao, got, out, direct, mirror):
@@ -437,15 +572,14 @@
 def shards(ao_blocks, block_live, tile_len, coeffs, metric_panel):
     pairs, ranks = lax.axis_size("pair"), lax.axis_size("aux")
     peers = pairs // PLANES
-    me, aux = lax.axis_index("pair"), lax.axis_index("aux")
+    me = lax.axis_index("pair")
     size, occ = coeffs.shape
     inside = jnp.arange(size, dtype=jnp.int32)
     valid = inside < lax.dynamic_index_in_dim(tile_len, me, 0, keepdims=False)
     turned = jnp.where(valid[None, :], jnp.transpose(coeffs), jnp.zeros((), coeffs.dtype))
-    part = lax.dynamic_slice_in_dim(turned, aux * (occ // ranks), occ // ranks, 0)
-    coefs = lax.all_gather(part[None], ("pair", "aux"), axis=0, tiled=True)
+    mine = turned.reshape(ranks, occ // ranks, size)
+    got, coefs = exchange(ao_blocks, mine, peers, ranks)
     coefs = coefs.reshape(pairs, occ, size)
-    got = exchange(ao_blocks, peers)
     parts = partials(ao_blocks, got, coefs, block_live, peers)
     slabs = ring(parts, peers, ranks)
     return fit(slabs, metric_panel, tile_len, occ // pairs)

time: 237 us -> 184 us (0.78)
  waiting for transfers between devices: 69.7 us -> 0 us
  Pallas kernels: 146 us -> 175 us
  between operations: 13.5 us -> 0.1 us
    all_gather x1 -> x0, waiting for transfers between devices: 69.7 us -> none  [shards(): coefs = lax.all_gather(part[None], ('pair', 'aux'), axis=0, tiled=True)]
    pallas_call x1, Pallas kernels: 54.4 us -> 81.4 us  [exchange(): pl.pallas_call(functools.partial(exchange_kernel, peers, ranks), out_shap...]
    pallas_call x1, Pallas kernels: 68.9 us -> 71.4 us  [ring(): pl.pallas_call(functools.partial(ring_kernel, peers, ranks), out_shape=ja...]
  transfers between devices with their start and end apart: 1 -> 0, of which waited for: 1 -> 0; matrix products, arithmetic and copies ran while one was open for 0% -> 0% of each run, Pallas kernels for 23% -> 0%
where the time goes in v3:
time: 184 us; the launch traced here: 183 us
  Pallas kernels  175 us (95%)
  local copies, waits for them, and re-layouts  5.48 us (3%)
  other arithmetic  2.51 us (1%)
    pallas_call x1, Pallas kernels, exchange(): pl.pallas_call(functools.partial(exchange_kernel, peers, ranks), out_shap...  81.4 us
    pallas_call x1, Pallas kernels, ring(): pl.pallas_call(functools.partial(ring_kernel, peers, ranks), out_shape=ja...  71.4 us
    pallas_call x1, Pallas kernels, partials(): pl.pallas_call(functools.partial(partial_kernel, peers), grid_spec=spec,...  19.9 us

profile of v3, /device:TPU:1, one launch (start us, length us, event | category | flops | bytes accessed | tf_op | source)
XLA Modules:
  0.0 183.3 jit_solution(7513609881551210571)
XLA Ops:
  0.0 0.1 pad_add_fusion.place
  0.1 1.2 dynamic_slice.8
  1.3 0.6 iota_compare_fusion.1
  2.0 1.6 broadcast_select_fusion
  3.6 0.0 copy-start.1
  3.6 81.4 %shard_map.55 = (bf16[8,8,4,64,128]{4,3,2,1,0:T(8,128)(2,1)}, bf16[8,8,4,144,128]{4,3,2,1,0:T(8,128)(2,1)}) custom-call(bf16[64,1,4,128,128]{4,3,2,1,0:T(8,128)(2,1)} %ao.3, bf16[4,144,128]{2,1,0:T(8,128)(2,1)} %bitcast.16), custom_call_target="tpu_custom_call" | custom-call | tf_op jit(solution)/shard_map/pallas_call | solution.py:189
  84.9 0.0 copy-done.1
  84.9 0.0 copy-start
  84.9 2.2 %copy-done = bf16[8,8,4,64,128]{4,3,2,1,0:T(8,128)(2,1)S(1)} copy-done((bf16[8,8,4,64,128]{4,3,2,1,0:T(8,128)(2,1)S(1)}, bf16[8,8,4,64,128]{4,3,2,1,0:T(8,128)(2,1)}, u32[]{:S(2)}) %copy-start) | copy-done | bytes 4194328
  87.1 19.9 %shard_map.56.parts = f32[8,8,2,144,128]{4,3,2,1,0:T(8,128)} custom-call(s32[2]{0:T(128)S(1)} %pad_add_fusion.place, s32[64,64]{1,0:T(8,128)S(1)} %copy-done.1, bf16[64,576,128]{2,1,0:T(8,128)(2,1)} %bitcast.14, bf16[64,576,128]{2,1,0:T(8,128)(2,1)} %bitcast.15, bf16[64,1,4,128,128]{4,3,2,1,0:T(8,128)(2,1)} %ao.3, bf16[8,8,4,64,128]{4,3,2,1,0:T(8,128)(2,1)S(1)} %copy-done), custom_call_target="tpu_custom_call" | custom-call | tf_op jit(solution)/shard_map/pallas_call | solution.py:334
  107.1 0.0 copy-start.3
  107.1 0.0 copy-start.2
  107.1 71.4 %shard_map.57.slabs = bf16[8,4,8,48,128]{4,3,2,1,0:T(8,128)(2,1)S(1)} custom-call(f32[8,8,2,144,128]{4,3,2,1,0:T(8,128)} %shard_map.56.parts), custom_call_target="tpu_custom_call" | custom-call | bytes 180000000 | tf_op jit(solution)/shard_map/pallas_call | solution.py:498
  178.5 0.0 copy-done.3
  178.5 0.1 dynamic-slice_convert_fusion
  178.5 0.1 fusion
  178.7 0.2 reshape.16
  178.9 0.1 copy.8.weights
  179.0 0.0 copy-done.2
  179.0 2.5 %shard_map.58 = bf16[8,9,8192]{2,1,0:T(8,128)(2,1)S(1)} custom-call(s32[64]{0:T(128)S(1)} %copy-done.2, bf16[128,192]{1,0:T(8,128)(2,1)S(1)} %copy.8.weights, bf16[8,4,8,48,128]{4,3,2,1,0:T(8,128)(2,1)S(1)} %shard_map.57.slabs), custom_call_target="tpu_custom_call" | custom-call | tf_op jit(solution)/shard_map/pallas_call | solution.py:564
  181.5 1.7 copy.9
  (2 shorter events, 0.0 us)
Async XLA Ops:
  3.6 81.4 %copy-start.1 = (s32[64,64]{1,0:T(8,128)S(1)}, s32[64,64]{1,0:T(8,128)}, u32[]{:S(2)}) copy-start(s32[64,64]{1,0:T(8,128)} %live.1) | copy-start | bytes 49156
  84.9 2.2 %copy-start = (bf16[8,8,4,64,128]{4,3,2,1,0:T(8,128)(2,1)S(1)}, bf16[8,8,4,64,128]{4,3,2,1,0:T(8,128)(2,1)}, u32[]{:S(2)}) copy-start(bf16[8,8,4,64,128]{4,3,2,1,0:T(8,128)(2,1)} %get-tuple-element.8.got) | copy-start | bytes 12582916
  107.1 71.4 %copy-start.3 = (bf16[16,32]{1,0:T(8,128)(2,1)S(1)}, bf16[16,32]{1,0:T(8,128)(2,1)}, u32[]{:S(2)}) copy-start(bf16[16,32]{1,0:T(8,128)(2,1)} %param.9) | copy-start | bytes 3076
  107.1 71.9 %copy-start.2 = (s32[64]{0:T(128)S(1)}, s32[64]{0:T(128)}, u32[]{:S(2)}) copy-start(s32[64]{0:T(128)} %lengths.1) | copy-start | bytes 772

commit v4 on v1

v4 whole, which is shorter than its diff:
```python
import functools

import jax
import jax.numpy as jnp
from jax import lax
from jax.experimental import pallas as pl
from jax.experimental.pallas import tpu as pltpu
from jax.sharding import PartitionSpec as P

MESH = pl.DeviceIdType.MESH
PLANES = 8
REACH = 4
F32 = jnp.float32
BF16 = jnp.bfloat16


def half_kernel(
    peers, ranks, live, lengths, coeffs, ao, out,
    mine, coefs, got, held, diagonal, wide_own, high_own, direct, mirror, own, sent, came,
    total, padded, sheet, seen,
    x_send, x_recv, x_own, held_sem, mine_sem, gz_send, gz_recv, gx_send, gx_recv, gy_send, gy_recv,
    gc_send, gc_recv, bx_send, bx_recv, bz_send, bz_recv, bc_send, bc_recv,
    send_sem, recv_sem, plane_send, plane_recv, line_send, line_recv, line_own,
):
    me, aux = lax.axis_index("pair"), lax.axis_index("aux")
    plane, slot = me // peers, me % peers
    chips = peers // 2
    chip, core = slot // 2, slot % 2
    slab, half, size = got.shape[2:]
    occ = mine.shape[0]
    low_rows = quarter_rows(occ, ranks)
    rest = pl.ds(low_rows * ranks, occ - low_rows * ranks)
    chunk = occ // PLANES
    share = chunk // peers
    begin = PLANES - 2

    def remote(src, dst, sends, recvs, device):
        return pltpu.make_async_remote_copy(
            src_ref=src, dst_ref=dst, send_sem=sends, recv_sem=recvs,
            device_id=device, device_id_type=MESH,
        )

    def shifted(move):
        return lax.rem(plane + move + PLANES, PLANES)

    def in_plane(step):
        return lax.rem(slot + step, peers)

    def in_line(step):
        return lax.rem(aux + step + ranks, ranks)

    def in_row(step):
        return lax.rem(chip + step + chips, chips)

    def quarter(rank):
        return pl.ds(pl.multiple_of(rank * low_rows, 16), low_rows)

    def gather_z(step):
        return remote(
            mine.at[quarter(aux)], coefs.at[plane, core, chip, quarter(aux)],
            gz_send.at[step], gz_recv.at[step], (shifted(step) * peers + slot, aux),
        )

    def batch(step, rank):
        return coefs.at[:, core, in_row(-step), quarter(rank)]

    def gather_x(step):
        return remote(
            batch(0, aux), batch(0, aux), gx_send.at[step], gx_recv.at[step],
            (plane * peers + in_row(step) * 2 + core, aux),
        )

    def gather_y(step, leg):
        way = 1 if leg == 0 or (leg == 2 and step % 2 == 0) else -1
        rank = aux if leg < 2 else in_line(-way)
        return remote(
            batch(step, rank), batch(step, rank), gy_send.at[step, leg], gy_recv.at[step, leg],
            (me, in_line(way)),
        )

    other_core = (me + 1 - 2 * core, aux)

    def gather_core(step, leg):
        rank = in_line((0, -1, 1, 2)[leg])
        return remote(
            batch(step, rank), batch(step, rank), gc_send.at[step, leg], gc_recv.at[step, leg],
            other_core,
        )

    def rest_x(step):
        return remote(
            mine.at[rest], coefs.at[plane, core, chip, rest], bx_send.at[step], bx_recv.at[step],
            (plane * peers + in_row(step) * 2 + core, aux),
        )

    def rest_z(way, count):
        sign = 1 if way == 0 else -1
        middle = max(chips // 2, 1)
        chunk_chips = pl.ds(0, chips)
        if count == REACH:
            chunk_chips = pl.ds(0, middle) if way == 0 else pl.ds(chips - middle, middle)
        part = coefs.at[shifted(-sign * (count - 1)), core, chunk_chips, rest]
        return remote(
            part, part, bz_send.at[way, count - 1], bz_recv.at[way, count - 1],
            (shifted(sign) * peers + slot, aux),
        )

    def rest_core(move):
        part = coefs.at[shifted(move), core, :, rest]
        return remote(
            part, part, bc_send.at[move + REACH - 1], bc_recv.at[move + REACH - 1], other_core
        )

    own_quarter = pltpu.make_async_copy(
        mine.at[quarter(aux)], coefs.at[plane, core, chip, quarter(aux)], mine_sem.at[0]
    )
    own_rest = pltpu.make_async_copy(
        mine.at[rest], coefs.at[plane, core, chip, rest], mine_sem.at[1]
    )

    def piece(tile):
        start = pl.multiple_of(jnp.where(tile > me, 0, half), half)
        return ao.at[tile, 0, :, pl.ds(start, half), :]

    def send(group, step):
        other = in_plane(step)
        return remote(
            piece(group * peers + other), got.at[group, slot],
            x_send.at[group, step], x_recv.at[group, step], (plane * peers + other, aux),
        )

    def keep(group):
        return pltpu.make_async_copy(
            piece(group * peers + slot), got.at[group, slot], x_own.at[group]
        )

    def hold(group, m):
        return pltpu.make_async_copy(
            piece(group * peers + m), held.at[group, m], held_sem.at[group, m]
        )

    hold_diagonal = pltpu.make_async_copy(ao.at[me, 0], diagonal, mine_sem.at[2])

    def hop(way, group, left):
        halves = pl.ds(way, 1) if left == REACH else pl.ds(0, 2)
        return remote(
            sent.at[way, group, left - 1, halves], came.at[way, group, left - 1, halves],
            send_sem.at[way, group, left - 1], recv_sem.at[way, group, left - 1],
            (shifted(1 if way == 0 else -1) * peers + slot, aux),
        )

    def spread(group, step):
        other = in_plane(step)
        return remote(
            sheet.at[group, other], seen.at[group, slot],
            plane_send.at[group, step], plane_recv.at[group, step], (plane * peers + other, aux),
        )

    def line(group, step):
        return remote(
            seen.at[group], out.at[group, aux], line_send.at[group, step], line_recv.at[group, step],
            (me, in_line(step)),
        )

    def line_keep(group):
        return pltpu.make_async_copy(seen.at[group], out.at[group, aux], line_own.at[group])

    barrier = pltpu.get_barrier_semaphore()

    def greet(device):
        pl.semaphore_signal(barrier, inc=1, device_id=device, device_id_type=MESH)

    for step in range(1, peers):
        greet((plane * peers + in_plane(step), aux))
    for step in range(1, PLANES):
        greet((shifted(step) * peers + slot, aux))
    for step in range(1, ranks):
        greet((me, in_line(step)))

    hold_diagonal.start()

    @pl.loop(0, PLANES)
    def _(group):
        for m in range(peers):
            hold(group, m).start()

    column = lax.broadcasted_iota(jnp.int32, (occ, size), 1)
    valid = jnp.where(column < lengths[me], 1.0, 0.0).astype(F32)
    mine[...] = (jnp.transpose(coeffs[...].astype(F32)) * valid).astype(BF16)
    padded[...] = jnp.zeros_like(padded)
    pl.semaphore_wait(barrier, peers - 1 + PLANES - 1 + ranks - 1)

    own_quarter.start()
    own_rest.start()
    for step in range(1, chips):
        rest_x(step).start()
    for step in range(1, PLANES):
        gather_z(step).start()

    def offer(step):
        gather_y(step, 0).start()
        gather_y(step, 1).start()
        gather_core(step, 0).start()

    def relay(step):
        gather_y(step, 0).wait_recv()
        gather_y(step, 1).wait_recv()
        gather_y(step, 2).start()
        gather_core(step, 1).start()
        gather_core(step, 2).start()

    def close(step):
        gather_y(step, 2).wait_recv()
        gather_core(step, 3).start()

    def rest_next(count):
        for way in range(2):
            rest_z(way, count).wait_recv()
        for way in range(2):
            if count < REACH:
                rest_z(way, count + 1).start()
        if count < REACH:
            rest_core(-count).start()
            rest_core(count).start()
        else:
            rest_core(REACH).start()

    def gather_turn(turn):
        @pl.when(turn == 1)
        def _():
            own_quarter.wait()
            own_rest.wait()
            for step in range(1, PLANES):
                gather_z(step).wait_recv()
            for step in range(1, chips):
                gather_x(step).start()
            offer(0)
            for step in range(1, chips):
                rest_x(step).wait_recv()
            rest_z(0, 1).start()
            rest_z(1, 1).start()
            rest_core(0).start()

        @pl.when(turn == 2)
        def _():
            for step in range(1, chips):
                gather_x(step).wait_recv()
                offer(step)
            rest_next(1)

        @pl.when(turn == 3)
        def _():
            for step in range(chips // 2):
                relay(step)
            rest_next(2)

        @pl.when(turn == 4)
        def _():
            for step in range(chips // 2):
                close(step)
            for step in range(chips // 2, chips):
                relay(step)
            rest_next(3)

        @pl.when(turn == 5)
        def _():
            for step in range(chips // 2, chips):
                close(step)
            rest_next(REACH)
            for step in range(chips):
                for leg in range(4):
                    gather_core(step, leg).wait_recv()
            for move in range(1 - REACH, REACH + 1):
                rest_core(move).wait_recv()

    def one(cond):
        return jnp.where(cond, 1.0, 0.0).astype(F32)

    def kept(first, second):
        return one(live[jnp.maximum(first, second), jnp.minimum(first, second)] > 0)

    def coef(group, m):
        return coefs[group, m % 2, m // 2]

    def wide(group):
        return jnp.concatenate([coef(group, m) for m in range(peers)], axis=1)

    def cut(group, start):
        return jnp.concatenate(
            [coef(group, m)[:, start : start + half] for m in range(peers)], axis=1
        )

    def straight(left, right):
        return lax.dot_general(left, right, (((1,), (0,)), ((), ())), preferred_element_type=F32)

    def turned(left, right):
        return lax.dot_general(left, right, (((1,), (1,)), ((), ())), preferred_element_type=F32)

    def scaled(block, factor):
        return block * jnp.full((half, size), factor, F32).astype(BF16)

    lower = lax.broadcasted_iota(jnp.int32, (occ, size), 1) < half

    def place(acc, result, upper):
        for p in range(slab):
            value = result[:, (p // 2) * size : (p // 2 + 1) * size]
            if (p % 2 == 0) == upper:
                value = pltpu.roll(value, half, 1)
            value = jnp.where(lower, 0.0, value) if upper else jnp.where(lower, value, 0.0)
            acc[:, p * size : (p + 1) * size] += value

    def stacked(source, group, factors):
        return jnp.concatenate(
            [
                jnp.concatenate([scaled(source[group, m, p], factors[m]) for p in range(slab)], axis=1)
                for m in range(peers)
            ],
            axis=0,
        )

    def beside(source, group, factors):
        return jnp.concatenate(
            [
                jnp.concatenate([scaled(source[group, m, p], factors[m]) for p in range(slab)], axis=0)
                for m in range(peers)
            ],
            axis=1,
        )

    def sum_direct():
        hold_diagonal.wait()
        row = lax.broadcasted_iota(jnp.int32, (size, size), 0)
        col = lax.broadcasted_iota(jnp.int32, (size, size), 1)
        factor = kept(me, me)
        tril = (factor * one(row >= col)).astype(BF16)
        strict = (factor * one(row > col)).astype(BF16)
        blocks = [diagonal[p] * tril for p in range(slab)]
        direct[...] = straight(mine[...], jnp.concatenate(blocks, axis=1))
        blocks = [diagonal[p] * strict for p in range(slab)]
        direct[...] += turned(mine[...], jnp.concatenate(blocks, axis=0))

        @pl.loop(0, PLANES)
        def _(group):
            for m in range(peers):
                hold(group, m).wait()

            @pl.when(group >= plane)
            def _():
                tiles = [group * peers + m for m in range(peers)]
                factors = [kept(tile, me) * one(tile > me) for tile in tiles]
                direct[...] += straight(cut(group, 0), stacked(held, group, factors))

            @pl.when(group <= plane)
            def _():
                tiles = [group * peers + m for m in range(peers)]
                factors = [kept(tile, me) * one(tile < me) for tile in tiles]
                place(direct, turned(wide(group), beside(held, group, factors)), True)

    def sum_mirror(group):
        keep(group).wait()
        for step in range(1, peers):
            send(group, step).wait_recv()
        target = group * peers + slot
        tiles = [plane * peers + m for m in range(peers)]

        @pl.when(group == plane)
        def _():
            mirror[...] = direct[...]

        @pl.when(group != plane)
        def _():
            mirror[...] = jnp.zeros_like(mirror)

        @pl.when(group >= plane)
        def _():
            factors = [kept(tile, target) * one(tile < target) for tile in tiles]
            place(mirror, turned(wide_own[...], beside(got, group, factors)), False)

        @pl.when(group <= plane)
        def _():
            factors = [kept(tile, target) * one(tile > target) for tile in tiles]
            mirror[...] += straight(high_own[...], stacked(got, group, factors))

        for z in range(PLANES):
            for p in range(slab):
                own[group, z, p // 2, (p % 2) * chunk : (p % 2 + 1) * chunk, :] = mirror[
                    z * chunk : (z + 1) * chunk, p * size : (p + 1) * size
                ]

    def pass_on(group, left):
        for way in range(2):
            goal = shifted(left if way == 0 else -left)
            if left == REACH:
                sent[way, group, left - 1, way] = own[group, goal, way].astype(BF16)
            else:
                hop(way, group, left + 1).wait_recv()
                for part in range(2):
                    value = own[group, goal, part]
                    if left < REACH - 1 or part == way:
                        value = value + came[way, group, left, part].astype(F32)
                    sent[way, group, left - 1, part] = value.astype(BF16)
            hop(way, group, left).start()

    def finish(group):
        for way in range(2):
            hop(way, group, 1).wait_recv()
        for part in range(2):
            total[part] = (
                own[group, plane, part]
                + came[0, group, 0, part].astype(F32)
                + came[1, group, 0, part].astype(F32)
            )
        for other in range(peers):
            for part in range(2):
                for odd in range(2):
                    start = odd * chunk + other * share
                    spot = (part * 2 + odd) * share
                    padded[other, spot : spot + share, :] = total[part, start : start + share, :]
            sheet[group, other] = padded[other].astype(BF16)
        seen[group, slot] = sheet[group, slot]
        for step in range(1, peers):
            spread(group, step).start()

    def along(group):
        for step in range(1, peers):
            spread(group, step).wait_recv()
        line_keep(group).start()
        for step in range(1, ranks):
            line(group, step).start()

    @pl.loop(0, begin + PLANES + REACH + 1)
    def _(turn):
        for left in range(1, REACH):
            group = turn - begin - (REACH - left)

            @pl.when((group >= 0) & (group < PLANES))
            def _(group=group, left=left):
                pass_on(group, left)

        gather_turn(turn)

        @pl.when(turn < PLANES)
        def _():
            keep(turn).start()
            for step in range(1, peers):
                send(turn, step).start()

        group = turn - begin - REACH

        @pl.when((group >= 0) & (group < PLANES))
        def _(group=group):
            finish(group)

        group = turn - begin - REACH - 1

        @pl.when((group >= 0) & (group < PLANES))
        def _(group=group):
            along(group)

        @pl.when(turn == begin)
        def _():
            wide_own[...] = wide(plane)
            high_own[...] = cut(plane, half)
            sum_direct()

        group = turn - begin

        @pl.when((group >= 0) & (group < PLANES))
        def _(group=group):
            sum_mirror(group)
            pass_on(group, REACH)

        @pl.when((turn >= 2) & (turn < PLANES + 2))
        def _():
            for step in range(1, peers):
                send(turn - 2, step).wait_send()

    for step in range(1, PLANES):
        gather_z(step).wait_send()
    for step in range(1, chips):
        gather_x(step).wait_send()
        rest_x(step).wait_send()
    for step in range(chips):
        for leg in range(3):
            gather_y(step, leg).wait_send()
        for leg in range(4):
            gather_core(step, leg).wait_send()
    for move in range(1 - REACH, REACH + 1):
        rest_core(move).wait_send()
    for way in range(2):
        for count in range(1, REACH + 1):
            rest_z(way, count).wait_send()

    @pl.loop(0, PLANES)
    def _(group):
        line_keep(group).wait()
        for step in range(1, ranks):
            line(group, step).wait()
        for step in range(1, peers):
            spread(group, step).wait_send()
        for way in range(2):
            for left in range(1, REACH + 1):
                hop(way, group, left).wait_send()


def quarter_rows(occ, ranks):
    return 16 * max(1, (occ * 5 // 9) // (16 * ranks))


def half_sums(ao, block_live, tile_len, coeffs, peers, ranks):
    _, _, slab, size, _ = ao.shape
    occ = coeffs.shape[1]
    chips = peers // 2
    rows = 2 * occ // PLANES
    room = -(-(2 * rows // peers) // 16) * 16
    dma = pltpu.SemaphoreType.DMA
    pieces = (PLANES, peers, slab, size // 2, size)
    hops = (2, PLANES, REACH)
    return pl.pallas_call(
        functools.partial(half_kernel, peers, ranks),
        out_shape=jax.ShapeDtypeStruct((PLANES, ranks, peers, room, size), BF16),
        in_specs=[
            pl.BlockSpec(memory_space=pltpu.SMEM),
            pl.BlockSpec(memory_space=pltpu.SMEM),
            pl.BlockSpec(memory_space=pltpu.VMEM),
            pl.BlockSpec(memory_space=pl.ANY),
        ],
        out_specs=pl.BlockSpec(memory_space=pl.ANY),
        scratch_shapes=[
            pltpu.VMEM((occ, size), BF16),
            pltpu.VMEM((PLANES, 2, chips, occ, size), BF16),
            pltpu.VMEM(pieces, BF16),
            pltpu.VMEM(pieces, BF16),
            pltpu.VMEM((slab, size, size), BF16),
            pltpu.VMEM((occ, peers * size), BF16),
            pltpu.VMEM((occ, peers * size // 2), BF16),
            pltpu.VMEM((occ, slab * size), F32),
            pltpu.VMEM((occ, slab * size), F32),
            pltpu.VMEM((PLANES, PLANES, 2, rows, size), F32),
            pltpu.VMEM(hops + (2, rows, size), BF16),
            pltpu.VMEM(hops + (2, rows, size), BF16),
            pltpu.VMEM((2, rows, size), F32),
            pltpu.VMEM((peers, room, size), F32),
            pltpu.VMEM((PLANES, peers, room, size), BF16),
            pltpu.VMEM((PLANES, peers, room, size), BF16),
            dma((PLANES, peers)), dma((PLANES, peers)), dma((PLANES,)), dma((PLANES, peers)), dma((3,)),
            dma((PLANES,)), dma((PLANES,)), dma((chips,)), dma((chips,)),
            dma((chips, 3)), dma((chips, 3)), dma((chips, 4)), dma((chips, 4)),
            dma((chips,)), dma((chips,)), dma((2, REACH)), dma((2, REACH)),
            dma((2 * REACH,)), dma((2 * REACH,)),
            dma(hops), dma(hops), dma((PLANES, peers)), dma((PLANES, peers)),
            dma((PLANES, ranks)), dma((PLANES, ranks)), dma((PLANES,)),
        ],
        compiler_params=pltpu.CompilerParams(
            collective_id=0, has_side_effects=True, vmem_limit_bytes=60 << 20
        ),
    )(block_live, tile_len, coeffs, ao)


def fit_kernel(peers, lengths, weights, slabs, out):
    group = pl.program_id(0)
    ranks, _, room, size = slabs.shape[1:]
    panel, share = out.shape[0], out.shape[1]
    inside = lax.broadcasted_iota(jnp.int32, (1, size), 1)
    blocks = [
        jnp.concatenate([slabs[0, r, m] for r in range(ranks)], axis=0) for m in range(peers)
    ]
    result = jnp.dot(
        weights[...], jnp.concatenate(blocks, axis=1), preferred_element_type=F32
    )
    for m in range(peers):
        valid = jnp.broadcast_to(inside < lengths[group * peers + m], (share, size))
        for q in range(panel):
            value = result[16 * q : 16 * q + share, m * size : (m + 1) * size]
            out[q, :, m * size : (m + 1) * size] = jnp.where(valid, value, 0.0).astype(BF16)


def fit(slabs, metric, tile_len, share):
    groups, ranks, peers, room, size = slabs.shape
    slab, panel_all = metric.shape
    panel = panel_all // ranks
    local = lax.dynamic_slice_in_dim(metric, lax.axis_index("aux") * panel, panel, 1)
    weights = jnp.einsum(
        "pq,ij->qipj", local.astype(F32), jnp.eye(16, share, dtype=F32)
    ).reshape(panel * 16, ranks, slab // ranks * share)
    weights = jnp.pad(weights, ((0, 0), (0, 0), (0, room - weights.shape[2])))
    weights = weights.reshape(panel * 16, ranks * room).astype(BF16)
    spec = pltpu.PrefetchScalarGridSpec(
        num_scalar_prefetch=1,
        grid=(groups,),
        in_specs=[
            pl.BlockSpec(weights.shape, lambda g, l: (0, 0)),
            pl.BlockSpec((1, ranks, peers, room, size), lambda g, l: (g, 0, 0, 0, 0)),
        ],
        out_specs=pl.BlockSpec((panel, share, peers * size), lambda g, l: (0, 0, g)),
    )
    return pl.pallas_call(
        functools.partial(fit_kernel, peers),
        grid_spec=spec,
        out_shape=jax.ShapeDtypeStruct((panel, share, groups * peers * size), BF16),
        compiler_params=pltpu.CompilerParams(vmem_limit_bytes=32 << 20),
    )(tile_len, weights, slabs)


def shards(ao_blocks, block_live, tile_len, coeffs, metric_panel):
    pairs, ranks = lax.axis_size("pair"), lax.axis_size("aux")
    peers = pairs // PLANES
    occ = coeffs.shape[1]
    slabs = half_sums(ao_blocks, block_live, tile_len, coeffs, peers, ranks)
    return fit(slabs, metric_panel, tile_len, occ // pairs)


def solution(mesh):
    in_specs = (P(None, "pair", "aux", None, None), P(), P(), P("pair", None), P())
    out_specs = P("aux", "pair", None)
    return jax.shard_map(shards, mesh=mesh, in_specs=in_specs, out_specs=out_specs, check_vma=False)
```

time: 314 us -> 140 us (0.45)
  waiting for transfers between devices: 170 us -> 0 us
  Pallas kernels: 0 us -> 133 us
  matrix products: 40.1 us -> 0 us
  local copies, waits for them, and re-layouts: 36.9 us -> 5.65 us
  blocking collectives: 25.4 us -> 0 us
  between operations: 13.6 us -> 0.07 us
  starting transfers between devices: 13.3 us -> 0 us
  other arithmetic: 14 us -> 0.88 us
    all_gather x2 -> x0, waiting for transfers between devices: 169 us -> none  [the longest x1 122 us: shards(): coef_rows = lax.all_gather(coeffs, 'pair', axis=0, tiled=True)]
    pallas_call x0 -> x2, Pallas kernels: none -> 133 us  [the longest x1 130 us: half_sums(): pl.pallas_call(functools.partial(half_kernel, peers, ranks), out_shape=ja...]
    dot_general x5 -> x0, matrix products: 40.1 us -> none  [the longest x1 10.4 us: shards(): jnp.einsum('kri,kgprs->pigs', coef_piece, own_stored, preferred_element_t...]
    all_to_all x1 -> x0, blocking collectives: 25.4 us -> none  [shards(): lax.all_to_all(half_done, 'pair', split_axis=1, concat_axis=2, tiled=True)]
    unnamed x12 -> x5, local copies, waits for them, and re-layouts: 24.3 us -> 3.6 us
    all_to_all x1 -> x0, starting transfers between devices: 13.3 us -> none  [receive_rows(): lax.all_to_all(needed, 'pair', split_axis=0, concat_axis=1, tiled=True)]
    slice x4 -> x0, local copies, waits for them, and re-layouts: 10.5 us -> none  [the longest x1 10.4 us: shards(): coef_piece[:, half_size:, :]]
    select_n x1 -> x0, other arithmetic: 5.11 us -> none  [receive_rows(): jnp.where(later, ao_blocks[:, :, :, :half_size], ao_blocks[:, :, :, half_...]
  transfers between devices with their start and end apart: 3 -> 0, of which waited for: 2 -> 0; matrix products, arithmetic and copies ran while one was open for 19% -> 0% of each run, Pallas kernels for 0% -> 0%
where the time goes in v4:
time: 140 us
  Pallas kernels  133 us (95%)
  local copies, waits for them, and re-layouts  5.65 us (4%)
    pallas_call x1, Pallas kernels, half_sums(): pl.pallas_call(functools.partial(half_kernel, peers, ranks), out_shape=ja...  130 us
    unnamed x5, local copies, waits for them, and re-layouts  3.6 us

profile of v4, /device:TPU:1, one launch (start us, length us, event | category | flops | bytes accessed | tf_op | source)
XLA Modules:
  0.0 139.5 jit_solution(1587397176933199826)
XLA Ops:
  0.0 0.8 dynamic-slice_convert_fusion
  0.8 1.7 %copy.9.coeffs = bf16[128,576]{1,0:T(8,128)(2,1)} copy(bf16[128,576]{0,1:T(8,128)(2,1)} %param.8) | data formatting | bytes 294912 | tf_op args[3]
  2.5 0.1 fusion
  2.6 0.2 reshape.6
  2.8 0.1 copy.10.weights
  2.9 0.0 copy-start.1
  2.9 130.4 %shard_map.55.slabs = bf16[8,4,8,48,128]{4,3,2,1,0:T(8,128)(2,1)} custom-call(s32[64,64]{1,0:T(8,128)} %live.1, s32[64]{0:T(128)} %lengths.3, bf16[128,576]{1,0:T(8,128)(2,1)} %copy.9.coeffs, bf16[64,1,4,128,128]{4,3,2,1,0:T(8,128)(2,1)} %ao.1), custom_call_target="tpu_custom_call" | custom-call | tf_op jit(solution)/shard_map/pallas_call | solution.py:519
  133.3 0.0 copy-done.1
  133.3 0.0 copy-start
  133.3 1.9 %copy-done = bf16[8,4,8,48,128]{4,3,2,1,0:T(8,128)(2,1)S(1)} copy-done((bf16[8,4,8,48,128]{4,3,2,1,0:T(8,128)(2,1)S(1)}, bf16[8,4,8,48,128]{4,3,2,1,0:T(8,128)(2,1)}, u32[]{:S(2)}) %copy-start) | copy-done | bytes 3145752
  135.2 2.6 %shard_map.56 = bf16[8,9,8192]{2,1,0:T(8,128)(2,1)S(1)} custom-call(s32[64]{0:T(128)S(1)} %copy-done.1, bf16[128,192]{1,0:T(8,128)(2,1)S(1)} %copy.10.weights, bf16[8,4,8,48,128]{4,3,2,1,0:T(8,128)(2,1)S(1)} %copy-done), custom_call_target="tpu_custom_call" | custom-call | tf_op jit(solution)/shard_map/pallas_call | solution.py:597
  137.8 1.7 %copy.11 = bf16[8,9,8192]{2,0,1:T(8,128)(2,1)} copy(bf16[8,9,8192]{2,1,0:T(8,128)(2,1)S(1)} %shard_map.56) | data formatting | bytes 2359296 | tf_op jit(solution)/shard_map/pallas_call | solution.py:597
  (2 shorter events, 0.0 us)
Async XLA Ops:
  2.9 130.4 %copy-start.1 = (s32[64]{0:T(128)S(1)}, s32[64]{0:T(128)}, u32[]{:S(2)}) copy-start(s32[64]{0:T(128)} %lengths.3) | copy-start | bytes 772
  133.3 1.9 %copy-start = (bf16[8,4,8,48,128]{4,3,2,1,0:T(8,128)(2,1)S(1)}, bf16[8,4,8,48,128]{4,3,2,1,0:T(8,128)(2,1)}, u32[]{:S(2)}) copy-start(bf16[8,4,8,48,128]{4,3,2,1,0:T(8,128)(2,1)} %shard_map.55.slabs) | copy-start | bytes 9437188

commit v5 on v4

--- a/solution.py
+++ b/solution.py
@@ -15,12 +15,12 @@
 
 
 def half_kernel(
-    peers, ranks, live, lengths, coeffs, ao, out,
-    mine, coefs, got, held, diagonal, wide_own, high_own, direct, mirror, own, sent, came,
-    total, padded, sheet, seen,
+    peers, ranks, live, lengths, coeffs, weights, ao, out,
+    mine, coefs, got, held, diagonal, wide_own, high_own, direct, turned_sum, mirror, own, sent, came,
+    total, padded, sheet, slabs,
     x_send, x_recv, x_own, held_sem, mine_sem, gz_send, gz_recv, gx_send, gx_recv, gy_send, gy_recv,
     gc_send, gc_recv, bx_send, bx_recv, bz_send, bz_recv, bc_send, bc_recv,
-    send_sem, recv_sem, plane_send, plane_recv, line_send, line_recv, line_own,
+    send_sem, recv_sem, plane_send, plane_recv, line_send, line_recv,
 ):
     me, aux = lax.axis_index("pair"), lax.axis_index("aux")
     plane, slot = me // peers, me % peers
@@ -32,7 +32,7 @@
     rest = pl.ds(low_rows * ranks, occ - low_rows * ranks)
     chunk = occ // PLANES
     share = chunk // peers
-    begin = PLANES - 2
+    begin = 5
 
     def remote(src, dst, sends, recvs, device):
         return pltpu.make_async_remote_copy(
@@ -93,23 +93,21 @@
             (plane * peers + in_row(step) * 2 + core, aux),
         )
 
-    def rest_z(way, count):
+    def ways(count, step):
+        return (0, 1) if count < REACH else ((0,) if step < chips // 2 else (1,))
+
+    def rest_z(way, count, step):
         sign = 1 if way == 0 else -1
-        middle = max(chips // 2, 1)
-        chunk_chips = pl.ds(0, chips)
-        if count == REACH:
-            chunk_chips = pl.ds(0, middle) if way == 0 else pl.ds(chips - middle, middle)
-        part = coefs.at[shifted(-sign * (count - 1)), core, chunk_chips, rest]
-        return remote(
-            part, part, bz_send.at[way, count - 1], bz_recv.at[way, count - 1],
+        part = coefs.at[shifted(-sign * (count - 1)), core, in_row(-step), rest]
+        return remote(
+            part, part, bz_send.at[way, count - 1, step], bz_recv.at[way, count - 1, step],
             (shifted(sign) * peers + slot, aux),
         )
 
-    def rest_core(move):
-        part = coefs.at[shifted(move), core, :, rest]
-        return remote(
-            part, part, bc_send.at[move + REACH - 1], bc_recv.at[move + REACH - 1], other_core
-        )
+    def rest_core(move, step):
+        part = coefs.at[shifted(move), core, in_row(-step), rest]
+        spot = move + REACH - 1
+        return remote(part, part, bc_send.at[spot, step], bc_recv.at[spot, step], other_core)
 
     own_quarter = pltpu.make_async_copy(
         mine.at[quarter(aux)], coefs.at[plane, core, chip, quarter(aux)], mine_sem.at[0]
@@ -152,18 +150,15 @@
     def spread(group, step):
         other = in_plane(step)
         return remote(
-            sheet.at[group, other], seen.at[group, slot],
+            sheet.at[group, other], slabs.at[group, aux, slot],
             plane_send.at[group, step], plane_recv.at[group, step], (plane * peers + other, aux),
         )
 
     def line(group, step):
         return remote(
-            seen.at[group], out.at[group, aux], line_send.at[group, step], line_recv.at[group, step],
-            (me, in_line(step)),
-        )
-
-    def line_keep(group):
-        return pltpu.make_async_copy(seen.at[group], out.at[group, aux], line_own.at[group])
+            slabs.at[group, aux], slabs.at[group, aux],
+            line_send.at[group, step], line_recv.at[group, step], (me, in_line(step)),
+        )
 
     barrier = pltpu.get_barrier_semaphore()
 
@@ -186,7 +181,7 @@
 
     column = lax.broadcasted_iota(jnp.int32, (occ, size), 1)
     valid = jnp.where(column < lengths[me], 1.0, 0.0).astype(F32)
-    mine[...] = (jnp.transpose(coeffs[...].astype(F32)) * valid).astype(BF16)
+    mine[...] = (coeffs[...].astype(F32) * valid).astype(BF16)
     padded[...] = jnp.zeros_like(padded)
     pl.semaphore_wait(barrier, peers - 1 + PLANES - 1 + ranks - 1)
 
@@ -213,65 +208,76 @@
         gather_y(step, 2).wait_recv()
         gather_core(step, 3).start()
 
-    def rest_next(count):
+    def rest_next(count, step):
+        for way in ways(count, step):
+            rest_z(way, count, step).wait_recv()
         for way in range(2):
-            rest_z(way, count).wait_recv()
-        for way in range(2):
-            if count < REACH:
-                rest_z(way, count + 1).start()
+            if count < REACH and way in ways(count + 1, step):
+                rest_z(way, count + 1, step).start()
         if count < REACH:
-            rest_core(-count).start()
-            rest_core(count).start()
+            rest_core(-count, step).start()
+            rest_core(count, step).start()
         else:
-            rest_core(REACH).start()
+            rest_core(REACH, step).start()
+
+    def rest_first(step):
+        if step > 0:
+            rest_x(step).wait_recv()
+        rest_z(0, 1, step).start()
+        rest_z(1, 1, step).start()
+        rest_core(0, step).start()
 
     def gather_turn(turn):
-        @pl.when(turn == 1)
-        def _():
+        @pl.when(turn == 0)
+        def _():
+            own_rest.wait()
+            rest_first(0)
             own_quarter.wait()
-            own_rest.wait()
             for step in range(1, PLANES):
                 gather_z(step).wait_recv()
             for step in range(1, chips):
                 gather_x(step).start()
             offer(0)
-            for step in range(1, chips):
-                rest_x(step).wait_recv()
-            rest_z(0, 1).start()
-            rest_z(1, 1).start()
-            rest_core(0).start()
-
-        @pl.when(turn == 2)
-        def _():
+            rest_next(1, 0)
+            for step in range(1, chips):
+                rest_first(step)
+            rest_next(2, 0)
+            relay(0)
+
+        @pl.when(turn == 1)
+        def _():
+            for step in range(1, chips):
+                rest_next(1, step)
             for step in range(1, chips):
                 gather_x(step).wait_recv()
                 offer(step)
-            rest_next(1)
+
+        @pl.when(turn == 2)
+        def _():
+            rest_next(3, 0)
+            close(0)
+            for step in range(1, chips):
+                rest_next(2, step)
 
         @pl.when(turn == 3)
         def _():
-            for step in range(chips // 2):
+            rest_next(REACH, 0)
+            for step in range(1, chips):
                 relay(step)
-            rest_next(2)
+            for step in range(1, chips):
+                rest_next(3, step)
 
         @pl.when(turn == 4)
         def _():
-            for step in range(chips // 2):
+            for step in range(1, chips):
+                rest_next(REACH, step)
+            for step in range(1, chips):
                 close(step)
-            for step in range(chips // 2, chips):
-                relay(step)
-            rest_next(3)
-
-        @pl.when(turn == 5)
-        def _():
-            for step in range(chips // 2, chips):
-                close(step)
-            rest_next(REACH)
             for step in range(chips):
                 for leg in range(4):
                     gather_core(step, leg).wait_recv()
-            for move in range(1 - REACH, REACH + 1):
-                rest_core(move).wait_recv()
+                for move in range(1 - REACH, REACH + 1):
+                    rest_core(move, step).wait_recv()
 
     def one(cond):
         return jnp.where(cond, 1.0, 0.0).astype(F32)
@@ -339,6 +345,8 @@
         blocks = [diagonal[p] * strict for p in range(slab)]
         direct[...] += turned(mine[...], jnp.concatenate(blocks, axis=0))
 
+        turned_sum[...] = jnp.zeros_like(turned_sum)
+
         @pl.loop(0, PLANES)
         def _(group):
             for m in range(peers):
@@ -354,7 +362,9 @@
             def _():
                 tiles = [group * peers + m for m in range(peers)]
                 factors = [kept(tile, me) * one(tile < me) for tile in tiles]
-                place(direct, turned(wide(group), beside(held, group, factors)), True)
+                turned_sum[...] += turned(wide(group), beside(held, group, factors))
+
+        place(direct, turned_sum[...], True)
 
     def sum_mirror(group):
         keep(group).wait()
@@ -417,33 +427,57 @@
                     spot = (part * 2 + odd) * share
                     padded[other, spot : spot + share, :] = total[part, start : start + share, :]
             sheet[group, other] = padded[other].astype(BF16)
-        seen[group, slot] = sheet[group, slot]
+        slabs[group, aux, slot] = sheet[group, slot]
         for step in range(1, peers):
             spread(group, step).start()
 
     def along(group):
         for step in range(1, peers):
             spread(group, step).wait_recv()
-        line_keep(group).start()
         for step in range(1, ranks):
             line(group, step).start()
 
-    @pl.loop(0, begin + PLANES + REACH + 1)
+    inside = lax.broadcasted_iota(jnp.int32, (1, size), 1)
+    panel = out.shape[1]
+
+    def fit(group):
+        for step in range(1, ranks):
+            line(group, step).wait_recv()
+        blocks = [
+            jnp.concatenate([slabs[group, r, m] for r in range(ranks)], axis=0)
+            for m in range(peers)
+        ]
+        result = straight(weights[...], jnp.concatenate(blocks, axis=1))
+        for m in range(peers):
+            valid = jnp.broadcast_to(inside < lengths[group * peers + m], (panel, size))
+            columns = pl.ds(pl.multiple_of((group * peers + m) * size, size), size)
+            for i in range(share):
+                value = result[panel * i : panel * (i + 1), m * size : (m + 1) * size]
+                out[i, :, columns] = jnp.where(valid, value, 0.0).astype(BF16)
+
+    @pl.loop(0, begin + PLANES + REACH + 4)
     def _(turn):
-        for left in range(1, REACH):
+        gather_turn(turn)
+
+        @pl.when(turn == begin)
+        def _():
+            wide_own[...] = wide(plane)
+            high_own[...] = cut(plane, half)
+            sum_direct()
+            sum_mirror(0)
+
+        for left in range(REACH, 0, -1):
             group = turn - begin - (REACH - left)
 
             @pl.when((group >= 0) & (group < PLANES))
             def _(group=group, left=left):
                 pass_on(group, left)
 
-        gather_turn(turn)
-
-        @pl.when(turn < PLANES)
-        def _():
-            keep(turn).start()
+        @pl.when((turn >= 1) & (turn <= PLANES))
+        def _():
+            keep(turn - 1).start()
             for step in range(1, peers):
-                send(turn, step).start()
+                send(turn - 1, step).start()
 
         group = turn - begin - REACH
 
@@ -451,29 +485,28 @@
         def _(group=group):
             finish(group)
 
-        group = turn - begin - REACH - 1
+        group = turn - begin - REACH - 2
 
         @pl.when((group >= 0) & (group < PLANES))
         def _(group=group):
             along(group)
 
-        @pl.when(turn == begin)
-        def _():
-            wide_own[...] = wide(plane)
-            high_own[...] = cut(plane, half)
-            sum_direct()
-
-        group = turn - begin
+        group = turn - begin - REACH - 4
 
         @pl.when((group >= 0) & (group < PLANES))
         def _(group=group):
+            fit(group)
+
+        group = turn - begin + 1
+
+        @pl.when((group >= 1) & (group < PLANES))
+        def _(group=group):
             sum_mirror(group)
-            pass_on(group, REACH)
-
-        @pl.when((turn >= 2) & (turn < PLANES + 2))
+
+        @pl.when((turn >= 4) & (turn < PLANES + 4))
         def _():
             for step in range(1, peers):
-                send(turn - 2, step).wait_send()
+                send(turn - 4, step).wait_send()
 
     for step in range(1, PLANES):
         gather_z(step).wait_send()
@@ -485,17 +518,16 @@
             gather_y(step, leg).wait_send()
         for leg in range(4):
             gather_core(step, leg).wait_send()
-    for move in range(1 - REACH, REACH + 1):
-        rest_core(move).wait_send()
-    for way in range(2):
+        for move in range(1 - REACH, REACH + 1):
+            rest_core(move, step).wait_send()
         for count in range(1, REACH + 1):
-            rest_z(way, count).wait_send()
+            for way in ways(count, step):
+                rest_z(way, count, step).wait_send()
 
     @pl.loop(0, PLANES)
     def _(group):
-        line_keep(group).wait()
         for step in range(1, ranks):
-            line(group, step).wait()
+            line(group, step).wait_send()
         for step in range(1, peers):
             spread(group, step).wait_send()
         for way in range(2):
@@ -507,25 +539,28 @@
     return 16 * max(1, (occ * 5 // 9) // (16 * ranks))
 
 
-def half_sums(ao, block_live, tile_len, coeffs, peers, ranks):
+def fitted_panel(ao, block_live, tile_len, coeffs, weights, room, peers, ranks):
     _, _, slab, size, _ = ao.shape
-    occ = coeffs.shape[1]
+    occ = coeffs.shape[0]
     chips = peers // 2
     rows = 2 * occ // PLANES
-    room = -(-(2 * rows // peers) // 16) * 16
+    share = occ // (PLANES * peers)
     dma = pltpu.SemaphoreType.DMA
     pieces = (PLANES, peers, slab, size // 2, size)
     hops = (2, PLANES, REACH)
     return pl.pallas_call(
         functools.partial(half_kernel, peers, ranks),
-        out_shape=jax.ShapeDtypeStruct((PLANES, ranks, peers, room, size), BF16),
+        out_shape=jax.ShapeDtypeStruct(
+            (share, weights.shape[0] // share, PLANES * peers * size), BF16
+        ),
         in_specs=[
             pl.BlockSpec(memory_space=pltpu.SMEM),
             pl.BlockSpec(memory_space=pltpu.SMEM),
             pl.BlockSpec(memory_space=pltpu.VMEM),
+            pl.BlockSpec(memory_space=pltpu.VMEM),
             pl.BlockSpec(memory_space=pl.ANY),
         ],
-        out_specs=pl.BlockSpec(memory_space=pl.ANY),
+        out_specs=pl.BlockSpec(memory_space=pltpu.VMEM),
         scratch_shapes=[
             pltpu.VMEM((occ, size), BF16),
             pltpu.VMEM((PLANES, 2, chips, occ, size), BF16),
@@ -535,6 +570,7 @@
             pltpu.VMEM((occ, peers * size), BF16),
             pltpu.VMEM((occ, peers * size // 2), BF16),
             pltpu.VMEM((occ, slab * size), F32),
+            pltpu.VMEM((occ, slab * size // 2), F32),
             pltpu.VMEM((occ, slab * size), F32),
             pltpu.VMEM((PLANES, PLANES, 2, rows, size), F32),
             pltpu.VMEM(hops + (2, rows, size), BF16),
@@ -542,72 +578,42 @@
             pltpu.VMEM((2, rows, size), F32),
             pltpu.VMEM((peers, room, size), F32),
             pltpu.VMEM((PLANES, peers, room, size), BF16),
-            pltpu.VMEM((PLANES, peers, room, size), BF16),
+            pltpu.VMEM((PLANES, ranks, peers, room, size), BF16),
             dma((PLANES, peers)), dma((PLANES, peers)), dma((PLANES,)), dma((PLANES, peers)), dma((3,)),
             dma((PLANES,)), dma((PLANES,)), dma((chips,)), dma((chips,)),
             dma((chips, 3)), dma((chips, 3)), dma((chips, 4)), dma((chips, 4)),
-            dma((chips,)), dma((chips,)), dma((2, REACH)), dma((2, REACH)),
-            dma((2 * REACH,)), dma((2 * REACH,)),
+            dma((chips,)), dma((chips,)), dma((2, REACH, chips)), dma((2, REACH, chips)),
+            dma((2 * REACH, chips)), dma((2 * REACH, chips)),
             dma(hops), dma(hops), dma((PLANES, peers)), dma((PLANES, peers)),
-            dma((PLANES, ranks)), dma((PLANES, ranks)), dma((PLANES,)),
+            dma((PLANES, ranks)), dma((PLANES, ranks)),
         ],
         compiler_params=pltpu.CompilerParams(
             collective_id=0, has_side_effects=True, vmem_limit_bytes=60 << 20
         ),
-    )(block_live, tile_len, coeffs, ao)
-
-
-def fit_kernel(peers, lengths, weights, slabs, out):
-    group = pl.program_id(0)
-    ranks, _, room, size = slabs.shape[1:]
-    panel, share = out.shape[0], out.shape[1]
-    inside = lax.broadcasted_iota(jnp.int32, (1, size), 1)
-    blocks = [
-        jnp.concatenate([slabs[0, r, m] for r in range(ranks)], axis=0) for m in range(peers)
-    ]
-    result = jnp.dot(
-        weights[...], jnp.concatenate(blocks, axis=1), preferred_element_type=F32
-    )
-    for m in range(peers):
-        valid = jnp.broadcast_to(inside < lengths[group * peers + m], (share, size))
-        for q in range(panel):
-            value = result[16 * q : 16 * q + share, m * size : (m + 1) * size]
-            out[q, :, m * size : (m + 1) * size] = jnp.where(valid, value, 0.0).astype(BF16)
-
-
-def fit(slabs, metric, tile_len, share):
-    groups, ranks, peers, room, size = slabs.shape
+    )(block_live, tile_len, coeffs, weights, ao)
+
+
+def fit_weights(metric, ranks, share, room):
     slab, panel_all = metric.shape
     panel = panel_all // ranks
     local = lax.dynamic_slice_in_dim(metric, lax.axis_index("aux") * panel, panel, 1)
     weights = jnp.einsum(
-        "pq,ij->qipj", local.astype(F32), jnp.eye(16, share, dtype=F32)
-    ).reshape(panel * 16, ranks, slab // ranks * share)
+        "pq,ij->iqpj", local.astype(F32), jnp.eye(share, dtype=F32)
+    ).reshape(share * panel, ranks, slab // ranks * share)
     weights = jnp.pad(weights, ((0, 0), (0, 0), (0, room - weights.shape[2])))
-    weights = weights.reshape(panel * 16, ranks * room).astype(BF16)
-    spec = pltpu.PrefetchScalarGridSpec(
-        num_scalar_prefetch=1,
-        grid=(groups,),
-        in_specs=[
-            pl.BlockSpec(weights.shape, lambda g, l: (0, 0)),
-            pl.BlockSpec((1, ranks, peers, room, size), lambda g, l: (g, 0, 0, 0, 0)),
-        ],
-        out_specs=pl.BlockSpec((panel, share, peers * size), lambda g, l: (0, 0, g)),
-    )
-    return pl.pallas_call(
-        functools.partial(fit_kernel, peers),
-        grid_spec=spec,
-        out_shape=jax.ShapeDtypeStruct((panel, share, groups * peers * size), BF16),
-        compiler_params=pltpu.CompilerParams(vmem_limit_bytes=32 << 20),
-    )(tile_len, weights, slabs)
+    return weights.reshape(share * panel, ranks * room).astype(BF16)
 
 
 def shards(ao_blocks, block_live, tile_len, coeffs, metric_panel):
     pairs, ranks = lax.axis_size("pair"), lax.axis_size("aux")
     peers = pairs // PLANES
-    occ = coeffs.shape[1]
-    slabs = half_sums(ao_blocks, block_live, tile_len, coeffs, peers, ranks)
-    return fit(slabs, metric_panel, tile_len, occ // pairs)
+    share = coeffs.shape[1] // pairs
+    room = -(-(metric_panel.shape[0] // ranks * share) // 16) * 16
+    weights = fit_weights(metric_panel, ranks, share, room)
+    fitted = fitted_panel(
+        ao_blocks, block_live, tile_len, jnp.transpose(coeffs), weights, room, peers, ranks
+    )
+    return jnp.transpose(fitted, (1, 0, 2))
 
 
 def solution(mesh):

time: 140 us -> 133 us (0.950)
  Pallas kernels: 133 us -> 128 us
  local copies, waits for them, and re-layouts: 5.65 us -> 4.25 us
    pallas_call x2 -> x1, Pallas kernels: 133 us -> 128 us  [fitted_panel(): pl.pallas_call(functools.partial(half_kernel, peers, ranks), out_shape=ja...]
    pallas_call x1 -> x0, local copies, waits for them, and re-layouts: 1.73 us -> none  [fit(): pl.pallas_call(functools.partial(fit_kernel, peers), grid_spec=spec, out_...]
where the time goes in v5:
time: 133 us
  Pallas kernels  128 us (96%)
  local copies, waits for them, and re-layouts  4.25 us (3%)
    pallas_call x1, Pallas kernels, fitted_panel(): pl.pallas_call(functools.partial(half_kernel, peers, ranks), out_shape=ja...  128 us
    unnamed x5, local copies, waits for them, and re-layouts  3.26 us

profile of v5, /device:TPU:1, one launch (start us, length us, event | category | flops | bytes accessed | tf_op | source)
XLA Modules:
  0.0 132.9 jit_solution(3559827869101877487)
XLA Ops:
  0.0 0.0 copy-start
  0.0 0.7 copy-done
  0.7 0.1 constant_dynamic-slice_fusion
  0.8 0.1 copy.13
  0.9 0.1 fusion
  1.0 0.2 reshape.6
  1.2 0.1 copy.14
  1.3 0.7 copy.12.weights
  2.0 128.5 %shard_map.55 = bf16[9,8,8192]{2,1,0:T(8,128)(2,1)} custom-call(s32[64,64]{1,0:T(8,128)} %live.1, s32[64]{0:T(128)} %lengths.1, bf16[576,128]{1,0:T(8,128)(2,1)} %bitcast.9, bf16[72,192]{1,0:T(8,128)(2,1)} %copy.12.weights, bf16[64,1,4,128,128]{4,3,2,1,0:T(8,128)(2,1)} %ao.1), custom_call_target="tpu_custom_call" | custom-call | tf_op jit(solution)/shard_map/pallas_call | solution.py:551
  130.5 2.4 %copy.16 = bf16[8,9,8192]{2,0,1:T(8,128)(2,1)} copy(bf16[8,9,8192]{2,0,1:T(8,128)(2,1)} %bitcast.7) | data formatting | bytes 2359296
  (3 shorter events, 0.0 us)
Async XLA Ops:
  0.0 0.7 copy-start

commit v6 on v5

--- a/solution.py
+++ b/solution.py
@@ -17,7 +17,7 @@
 def half_kernel(
     peers, ranks, live, lengths, coeffs, weights, ao, out,
     mine, coefs, got, held, diagonal, wide_own, high_own, direct, turned_sum, mirror, own, sent, came,
-    total, padded, sheet, slabs,
+    total, padded, sheet, seen, loose, wall, slabs,
     x_send, x_recv, x_own, held_sem, mine_sem, gz_send, gz_recv, gx_send, gx_recv, gy_send, gy_recv,
     gc_send, gc_recv, bx_send, bx_recv, bz_send, bz_recv, bc_send, bc_recv,
     send_sem, recv_sem, plane_send, plane_recv, line_send, line_recv,
@@ -32,6 +32,7 @@
     rest = pl.ds(low_rows * ranks, occ - low_rows * ranks)
     chunk = occ // PLANES
     share = chunk // peers
+    tight = slab * share
     begin = 5
 
     def remote(src, dst, sends, recvs, device):
@@ -150,14 +151,18 @@
     def spread(group, step):
         other = in_plane(step)
         return remote(
-            sheet.at[group, other], slabs.at[group, aux, slot],
+            sheet.at[group, other], seen.at[group, slot],
             plane_send.at[group, step], plane_recv.at[group, step], (plane * peers + other, aux),
         )
 
-    def line(group, step):
-        return remote(
-            slabs.at[group, aux], slabs.at[group, aux],
-            line_send.at[group, step], line_recv.at[group, step], (me, in_line(step)),
+    def line(group, leg):
+        way = 1 if leg % 2 == 0 else -1
+        rank = aux if leg < 2 else in_line(-way)
+        rows = slabs.shape[2]
+        part = pl.ds(0, rows) if leg < 2 else pl.ds((leg - 2) * (rows // 2), rows // 2)
+        return remote(
+            slabs.at[group, rank, part], slabs.at[group, rank, part],
+            line_send.at[group, leg], line_recv.at[group, leg], (me, in_line(way)),
         )
 
     barrier = pltpu.get_barrier_semaphore()
@@ -427,26 +432,36 @@
                     spot = (part * 2 + odd) * share
                     padded[other, spot : spot + share, :] = total[part, start : start + share, :]
             sheet[group, other] = padded[other].astype(BF16)
-        slabs[group, aux, slot] = sheet[group, slot]
+        seen[group, slot] = sheet[group, slot]
         for step in range(1, peers):
             spread(group, step).start()
 
     def along(group):
         for step in range(1, peers):
             spread(group, step).wait_recv()
-        for step in range(1, ranks):
-            line(group, step).start()
+        for m in range(peers):
+            loose[m * tight : (m + 1) * tight, :] = seen[group, m].astype(F32)[:tight, :]
+        slabs[group, aux] = loose[...].astype(BF16)
+        line(group, 0).start()
+        line(group, 1).start()
+
+    def relay_line(group):
+        for leg in range(2):
+            line(group, leg).wait_recv()
+        for leg in range(2, 4):
+            line(group, leg).start()
 
     inside = lax.broadcasted_iota(jnp.int32, (1, size), 1)
     panel = out.shape[1]
 
     def fit(group):
-        for step in range(1, ranks):
-            line(group, step).wait_recv()
-        blocks = [
-            jnp.concatenate([slabs[group, r, m] for r in range(ranks)], axis=0)
-            for m in range(peers)
-        ]
+        for leg in range(2, 4):
+            line(group, leg).wait_recv()
+        for r in range(ranks):
+            loose[...] = slabs[group, r].astype(F32)
+            for m in range(peers):
+                wall[m, r * tight : (r + 1) * tight, :] = loose[m * tight : (m + 1) * tight, :]
+        blocks = [wall[m].astype(BF16) for m in range(peers)]
         result = straight(weights[...], jnp.concatenate(blocks, axis=1))
         for m in range(peers):
             valid = jnp.broadcast_to(inside < lengths[group * peers + m], (panel, size))
@@ -455,7 +470,7 @@
                 value = result[panel * i : panel * (i + 1), m * size : (m + 1) * size]
                 out[i, :, columns] = jnp.where(valid, value, 0.0).astype(BF16)
 
-    @pl.loop(0, begin + PLANES + REACH + 4)
+    @pl.loop(0, begin + PLANES + REACH + 3)
     def _(turn):
         gather_turn(turn)
 
@@ -473,25 +488,31 @@
             def _(group=group, left=left):
                 pass_on(group, left)
 
-        @pl.when((turn >= 1) & (turn <= PLANES))
-        def _():
-            keep(turn - 1).start()
-            for step in range(1, peers):
-                send(turn - 1, step).start()
-
         group = turn - begin - REACH
 
         @pl.when((group >= 0) & (group < PLANES))
         def _(group=group):
             finish(group)
 
-        group = turn - begin - REACH - 2
+        group = turn - begin - REACH - 1
 
         @pl.when((group >= 0) & (group < PLANES))
         def _(group=group):
             along(group)
 
-        group = turn - begin - REACH - 4
+        @pl.when((turn >= 0) & (turn < PLANES))
+        def _():
+            keep(turn).start()
+            for step in range(1, peers):
+                send(turn, step).start()
+
+        group = turn - begin - REACH - 2
+
+        @pl.when((group >= 0) & (group < PLANES))
+        def _(group=group):
+            relay_line(group)
+
+        group = turn - begin - REACH - 3
 
         @pl.when((group >= 0) & (group < PLANES))
         def _(group=group):
@@ -526,8 +547,8 @@
 
     @pl.loop(0, PLANES)
     def _(group):
-        for step in range(1, ranks):
-            line(group, step).wait_send()
+        for leg in range(4):
+            line(group, leg).wait_send()
         for step in range(1, peers):
             spread(group, step).wait_send()
         for way in range(2):
@@ -578,14 +599,17 @@
             pltpu.VMEM((2, rows, size), F32),
             pltpu.VMEM((peers, room, size), F32),
             pltpu.VMEM((PLANES, peers, room, size), BF16),
-            pltpu.VMEM((PLANES, ranks, peers, room, size), BF16),
+            pltpu.VMEM((PLANES, peers, room, size), BF16),
+            pltpu.VMEM((peers * slab * share, size), F32),
+            pltpu.VMEM((peers, ranks * slab * share, size), F32),
+            pltpu.VMEM((PLANES, ranks, peers * slab * share, size), BF16),
             dma((PLANES, peers)), dma((PLANES, peers)), dma((PLANES,)), dma((PLANES, peers)), dma((3,)),
             dma((PLANES,)), dma((PLANES,)), dma((chips,)), dma((chips,)),
             dma((chips, 3)), dma((chips, 3)), dma((chips, 4)), dma((chips, 4)),
             dma((chips,)), dma((chips,)), dma((2, REACH, chips)), dma((2, REACH, chips)),
             dma((2 * REACH, chips)), dma((2 * REACH, chips)),
             dma(hops), dma(hops), dma((PLANES, peers)), dma((PLANES, peers)),
-            dma((PLANES, ranks)), dma((PLANES, ranks)),
+            dma((PLANES, 4)), dma((PLANES, 4)),
         ],
         compiler_params=pltpu.CompilerParams(
             collective_id=0, has_side_effects=True, vmem_limit_bytes=60 << 20
@@ -593,15 +617,12 @@
     )(block_live, tile_len, coeffs, weights, ao)
 
 
-def fit_weights(metric, ranks, share, room):
+def fit_weights(metric, ranks, share):
     slab, panel_all = metric.shape
     panel = panel_all // ranks
     local = lax.dynamic_slice_in_dim(metric, lax.axis_index("aux") * panel, panel, 1)
-    weights = jnp.einsum(
-        "pq,ij->iqpj", local.astype(F32), jnp.eye(share, dtype=F32)
-    ).reshape(share * panel, ranks, slab // ranks * share)
-    weights = jnp.pad(weights, ((0, 0), (0, 0), (0, room - weights.shape[2])))
-    return weights.reshape(share * panel, ranks * room).astype(BF16)
+    weights = jnp.einsum("pq,ij->iqpj", local.astype(F32), jnp.eye(share, dtype=F32))
+    return weights.reshape(share * panel, slab * share).astype(BF16)
 
 
 def shards(ao_blocks, block_live, tile_len, coeffs, metric_panel):
@@ -609,7 +630,7 @@
     peers = pairs // PLANES
     share = coeffs.shape[1] // pairs
     room = -(-(metric_panel.shape[0] // ranks * share) // 16) * 16
-    weights = fit_weights(metric_panel, ranks, share, room)
+    weights = fit_weights(metric_panel, ranks, share)
     fitted = fitted_panel(
         ao_blocks, block_live, tile_len, jnp.transpose(coeffs), weights, room, peers, ranks
     )

time: 133 us -> 126 us (0.947)
  Pallas kernels: 128 us -> 121 us
    pallas_call x1, Pallas kernels: 128 us -> 121 us  [fitted_panel(): pl.pallas_call(functools.partial(half_kernel, peers, ranks), out_shape=ja...]
    unnamed x5 -> x4, local copies, waits for them, and re-layouts: 3.26 us -> 3.13 us
where the time goes in v6:
time: 126 us
  Pallas kernels  121 us (96%)
  local copies, waits for them, and re-layouts  4.12 us (3%)
    pallas_call x1, Pallas kernels, fitted_panel(): pl.pallas_call(functools.partial(half_kernel, peers, ranks), out_shape=ja...  121 us
    unnamed x4, local copies, waits for them, and re-layouts  3.13 us

profile of v6, /device:TPU:1, one launch (start us, length us, event | category | flops | bytes accessed | tf_op | source)
XLA Modules:
  0.0 125.6 jit_solution(5527803351021506440)
XLA Ops:
  0.0 0.0 copy-start
  0.0 0.7 copy-done
  0.7 0.1 constant_dynamic-slice_fusion
  0.8 0.1 copy.9
  0.9 0.1 fusion
  1.0 0.9 convert_element_type.11.weights
  1.9 121.3 %shard_map.55 = bf16[9,8,8192]{2,1,0:T(8,128)(2,1)} custom-call(s32[64,64]{1,0:T(8,128)} %live.1, s32[64]{0:T(128)} %lengths.1, bf16[576,128]{1,0:T(8,128)(2,1)} %bitcast.7, bf16[72,144]{1,0:T(8,128)(2,1)} %convert_element_type.11.weights, bf16[64,1,4,128,128]{4,3,2,1,0:T(8,128)(2,1)} %ao.1), custom_call_target="tpu_custom_call" | custom-call | tf_op jit(solution)/shard_map/pallas_call | solution.py:572
  123.3 2.4 %copy.11 = bf16[8,9,8192]{2,0,1:T(8,128)(2,1)} copy(bf16[8,9,8192]{2,0,1:T(8,128)(2,1)} %bitcast.6) | data formatting | bytes 2359296
  (2 shorter events, 0.0 us)
Async XLA Ops:
  0.0 0.7 copy-start

commit v7 on v6

--- a/solution.py
+++ b/solution.py
@@ -243,6 +243,9 @@
             for step in range(1, chips):
                 gather_x(step).start()
             offer(0)
+            keep(0).start()
+            for step in range(1, peers):
+                send(0, step).start()
             rest_next(1, 0)
             for step in range(1, chips):
                 rest_first(step)
@@ -500,11 +503,11 @@
         def _(group=group):
             along(group)
 
-        @pl.when((turn >= 0) & (turn < PLANES))
-        def _():
-            keep(turn).start()
+        @pl.when(turn < PLANES - 1)
+        def _():
+            keep(turn + 1).start()
             for step in range(1, peers):
-                send(turn, step).start()
+                send(turn + 1, step).start()
 
         group = turn - begin - REACH - 2
 

time: 126 us -> 126 us (level)
  no operation moved by 1% of the time
where the time goes in v7:
time: 126 us
  Pallas kernels  121 us (96%)
  local copies, waits for them, and re-layouts  4.12 us (3%)
    pallas_call x1, Pallas kernels, fitted_panel(): pl.pallas_call(functools.partial(half_kernel, peers, ranks), out_shape=ja...  121 us
    unnamed x4, local copies, waits for them, and re-layouts  3.13 us

profile of v7, /device:TPU:1, one launch (start us, length us, event | category | flops | bytes accessed | tf_op | source)
XLA Modules:
  0.0 125.7 jit_solution(6261526527131821327)
XLA Ops:
  0.0 0.0 copy-start
  0.0 0.7 copy-done
  0.7 0.1 constant_dynamic-slice_fusion
  0.8 0.1 copy.9
  0.9 0.1 fusion
  1.0 0.9 convert_element_type.11.weights
  1.9 121.4 %shard_map.55 = bf16[9,8,8192]{2,1,0:T(8,128)(2,1)} custom-call(s32[64,64]{1,0:T(8,128)} %live.1, s32[64]{0:T(128)} %lengths.1, bf16[576,128]{1,0:T(8,128)(2,1)} %bitcast.7, bf16[72,144]{1,0:T(8,128)(2,1)} %convert_element_type.11.weights, bf16[64,1,4,128,128]{4,3,2,1,0:T(8,128)(2,1)} %ao.1), custom_call_target="tpu_custom_call" | custom-call | tf_op jit(solution)/shard_map/pallas_call | solution.py:575
  123.3 2.4 %copy.11 = bf16[8,9,8192]{2,0,1:T(8,128)(2,1)} copy(bf16[8,9,8192]{2,0,1:T(8,128)(2,1)} %bitcast.6) | data formatting | bytes 2359296
  (2 shorter events, 0.0 us)
Async XLA Ops:
  0.0 0.7 copy-start
